TPU v7x, 128 devices: a whole 4x4x4 slice. The times are simulated.
128 devices in a mesh: lev: 8 (over y_lo, x), tile: 16 (over z, y_hi, core).
Axes of the slice: x: 4, y: 4 (y_hi: 2, y_lo: 2; y = y_hi * 2 + y_lo), z: 4, core: 2. Of those that a mesh axis runs over, the one named last changes fastest.
Arguments:
- inputs: bfloat16 [8, 80, 512, 128], P('lev', None, 'tile'), may hold values from -6 to 6
- level_ids: int32 [8], replicated, may hold values from 0 to 12
- level_table: bfloat16 [13, 512], replicated, may hold values from -6 to 6
- w_embed: bfloat16 [80, 512], replicated, may hold values from -0.625 to 0.625
- queries: bfloat16 [3, 512], replicated, may hold values from -6 to 6
- w_kv: bfloat16 [512, 1024], replicated, may hold values from -0.25 to 0.25
- w_out: bfloat16 [512, 512], replicated, may hold values from -0.25 to 0.25
- gain: float32 [512], replicated, may hold values from 0.1 to 1.9
- w_qkv: bfloat16 [512, 1536], replicated, may hold values from -0.25 to 0.25
- w_proj: bfloat16 [512, 512], replicated, may hold values from -0.25 to 0.25
- d_latent: bfloat16 [512, 128, 3, 512], P('tile', 'lev'), may hold values from -6 to 6
Outputs:
- swin_out: bfloat16 [512, 128, 3, 512], P('tile', 'lev')
- grad_embed: float32 [80, 512], replicated
- grad_keyval: float32 [512, 1024], replicated
- grad_out: float32 [512, 512], replicated
All inputs are finite; a program needn't handle non-finite values.
Results may differ from a plain program's by a relative error of at most 0.015.
Values may be sent and summed in bfloat16 or wider, within the bound.
A program may use at most 192 MiB of HBM per device.

v0:
```python
import functools
import math

import jax
import jax.numpy as jnp
import numpy as np
from jax import lax
from jax.experimental import pallas as pl
from jax.experimental.pallas import tpu as pltpu
from jax.sharding import PartitionSpec as P

HD = 64
HEADS = 8
WIN = 8
D = 512
F = 80
LEVELS = 8
LATENT = 3
KX = 128
MV = 544
CHUNK = 176
TERMS = 16 * CHUNK
BF = jnp.bfloat16
F32 = jnp.float32
VMEM_LIMIT = 56 * 1024 * 1024


def dot(a, b, ca=1, cb=0):
    return lax.dot_general(a, b, (((ca,), (cb,)), ((), ())), preferred_element_type=F32)


def split(value):
    high = value.astype(BF)
    return high, (value - high.astype(F32)).astype(BF)


def query_rows(queries):
    rows = jnp.concatenate([jnp.broadcast_to(queries[q : q + 1], (HEADS, D)) for q in range(LATENT)], axis=0)
    head = lax.broadcasted_iota(jnp.int32, (LATENT * HEADS, D), 0) % HEADS
    lane = lax.broadcasted_iota(jnp.int32, (LATENT * HEADS, D), 1) // HD
    return jnp.where(head == lane, rows, 0.0)


def weights_kernel(we_ref, queries_ref, wkv_ref, wout_ref, w2_ref, woutp_ref):
    row = lax.broadcasted_iota(jnp.int32, (D, D), 0)
    lane = lax.broadcasted_iota(jnp.int32, (D, D), 1)
    mix = jnp.where(lane == (row % HEADS) * HD + row // HEADS, 1.0, 0.0).astype(BF)
    we = we_ref[...]
    wv = dot(mix, wkv_ref[:, D:], 1, 1).astype(BF)
    woutp_ref[...] = dot(mix, wout_ref[...]).astype(BF)
    high, low = split(dot(wv, we, 1, 1))
    w2_ref[0:D, 0:KX] = high
    w2_ref[0:D, KX:] = low
    qm = query_rows(queries_ref[...].astype(F32)).astype(BF)
    shigh, slow = split(dot(qm, wkv_ref[:, :D], 1, 1) * (1.0 / math.sqrt(HD)))
    score = dot(shigh, we, 1, 1) + dot(slow, we, 1, 1)
    score = jnp.concatenate([score, jnp.zeros((MV - D - 24, KX), F32)], axis=0)
    high, low = split(score)
    w2_ref[D:MV, 0:KX] = high
    w2_ref[D:MV, KX:] = low


def level_rows(x, level):
    row = lax.broadcasted_iota(jnp.int32, (KX - F, 128), 0)
    ones = jnp.where(row == level, 1.0, 0.0).astype(BF)
    return jnp.concatenate([x, ones], axis=0)


def forward_levels(read, w2_ref, vals_ref):
    scores = []
    pairs = []
    for pair in range(LEVELS // 2):
        pixels = jnp.concatenate([level_rows(read(2 * pair), 2 * pair), level_rows(read(2 * pair + 1), 2 * pair + 1)], axis=1)
        pairs.append(pixels)
        out = dot(w2_ref[...], jnp.concatenate([pixels, pixels], axis=0))
        vals_ref[2 * pair] = out[:D, :128]
        vals_ref[2 * pair + 1] = out[:D, 128:]
        scores.append(out[D : D + 24, :128])
        scores.append(out[D : D + 24, 128:])
    expo = [jnp.exp(s) for s in scores]
    total = expo[0]
    for e in expo[1:]:
        total = total + e
    inverse = 1.0 / total
    return pairs, [(e * inverse).astype(BF).astype(F32) for e in expo]


def pool_kernel(x_ref, d_ref, w2_ref, woutp_ref, latent_ref, terms_ref, vals_ref, dpool_ref, pooled_ref, dv_ref, tacc_ref, gacc_ref):
    step = pl.program_id(0)
    pairs, probs = forward_levels(lambda l: x_ref[l], w2_ref, vals_ref)
    d_rows = jnp.concatenate([d_ref[:, q].reshape(128, D) for q in range(LATENT)], axis=0)
    dpool_ref[...] = dot(woutp_ref[...], d_rows, 1, 1)
    parts = [[probs[l][q * HEADS : (q + 1) * HEADS] for q in range(LATENT)] for l in range(LEVELS)]

    def mix_loop(i, carry):
        base = pl.multiple_of(i * 16, 16)
        pooled = [[], [], []]
        dvals = [[] for _ in range(LEVELS)]
        for e in range(2):
            rows = pl.ds(base + 8 * e, 8)
            dq = [dpool_ref[rows, q * 128 : (q + 1) * 128] for q in range(LATENT)]
            acc = [None] * LATENT
            for l in range(LEVELS):
                v = vals_ref[l, rows, :]
                for q in range(LATENT):
                    term = parts[l][q] * v
                    acc[q] = term if acc[q] is None else acc[q] + term
                dvals[l].append(parts[l][0] * dq[0] + parts[l][1] * dq[1] + parts[l][2] * dq[2])
            for q in range(LATENT):
                pooled[q].append(acc[q])
        for q in range(LATENT):
            pooled_ref[pl.ds(base, 16), q * 128 : (q + 1) * 128] = jnp.concatenate(pooled[q], axis=0).astype(BF)
        for l in range(LEVELS):
            lanes = slice((l % 2) * 128, (l % 2) * 128 + 128)
            dv_ref[l // 2, pl.ds(base, 16), lanes] = jnp.concatenate(dvals[l], axis=0).astype(BF)
        return carry

    lax.fori_loop(0, D // 16, mix_loop, 0)

    def dprob_loop(i, carry):
        acc = list(carry)
        for e in range(2):
            rows = pl.ds(pl.multiple_of(i * 16 + 8 * e, 8), 8)
            dq = [dpool_ref[rows, q * 128 : (q + 1) * 128] for q in range(LATENT)]
            for l in range(LEVELS):
                v = vals_ref[l, rows, :]
                for q in range(LATENT):
                    acc[l * LATENT + q] = acc[l * LATENT + q] + dq[q] * v
        return tuple(acc)

    zero = jnp.zeros((HEADS, 128), F32)
    dprob = lax.fori_loop(0, D // 16, dprob_loop, (zero,) * (LEVELS * LATENT))
    scale = 1.0 / math.sqrt(HD)
    delta = []
    for q in range(LATENT):
        total = parts[0][q] * dprob[q]
        for l in range(1, LEVELS):
            total = total + parts[l][q] * dprob[l * LATENT + q]
        delta.append(total)
    for l in range(LEVELS):
        ds = [parts[l][q] * (dprob[l * LATENT + q] - delta[q]) * scale for q in range(LATENT)]
        lanes = slice((l % 2) * 128, (l % 2) * 128 + 128)
        dv_ref[l // 2, D:MV, lanes] = jnp.concatenate(ds + [zero], axis=0).astype(BF)

    @pl.when(step == 0)
    def _():
        tacc_ref[...] = jnp.zeros_like(tacc_ref)
        gacc_ref[...] = jnp.zeros_like(gacc_ref)

    terms = dot(dv_ref[0], pairs[0], 1, 1)
    for pair in range(1, LEVELS // 2):
        terms = terms + dot(dv_ref[pair], pairs[pair], 1, 1)
    tacc_ref[...] += terms
    pooled = pooled_ref[...]
    gterm = dot(pooled, d_rows)
    for j in range(4):
        gacc_ref[j * D : (j + 1) * D, :] += gterm[:, j * 128 : (j + 1) * 128]
    latent = dot(pooled, woutp_ref[...], 0, 0).astype(BF)
    for q in range(LATENT):
        latent_ref[:, q] = latent[q * 128 : (q + 1) * 128].reshape(8, 16, D)

    @pl.when(step == pl.num_programs(0) - 1)
    def _():
        for h in range(HEADS):
            for j in range(4):
                terms_ref[j * D + h * HD : j * D + (h + 1) * HD, :] = gacc_ref[pl.ds(j * D + h, HD, stride=HEADS), :].astype(BF)
            terms_ref[4 * D + h * HD : 4 * D + (h + 1) * HD, :] = tacc_ref[pl.ds(h, HD, stride=HEADS), :].astype(BF)
        terms_ref[5 * D : 5 * D + MV - D, :] = tacc_ref[D:MV, :].astype(BF)
        terms_ref[5 * D + MV - D :, :] = jnp.zeros((TERMS - 5 * D - MV + D, KX), BF)


def normalise(values, gain):
    mean = jnp.mean(values, axis=-1, keepdims=True)
    centred = values - mean
    var = jnp.mean(centred * centred, axis=-1, keepdims=True)
    return (centred * lax.rsqrt(var + 1e-05) * gain).astype(BF)


def window_index(column, wa):
    return column * 3 + wa


def permutation(rows, dim):
    dst = lax.broadcasted_iota(jnp.int32, (rows, rows), dim)
    src = lax.broadcasted_iota(jnp.int32, (rows, rows), 1 - dim)
    a = dst
    b = dst - 96
    c = dst - 288
    low = (a // 4) * 16 + a % 4
    mid = (b // 8) * 16 + 4 + b % 8
    high = (c // 4) * 16 + 12 + c % 4
    want = jnp.where(dst < 96, low, jnp.where(dst < 288, mid, high))
    return jnp.where(src == want, 1.0, 0.0).astype(BF)


def window_kernel(edge_ref, xh_ref, latent_ref, w2_ref, woutp_ref, gain_ref, wqkv_ref, wproj_ref, out_ref, vals_ref, pooled_ref, q_ref, kv_ref, att_ref):
    gain = gain_ref[...]

    def halo(group, carry):
        lane0 = pl.multiple_of(group * 128, 128)
        _, probs = forward_levels(lambda l: xh_ref[l, :, pl.ds(lane0, 128)], w2_ref, vals_ref)
        parts = [[probs[l][q * HEADS : (q + 1) * HEADS] for q in range(LATENT)] for l in range(LEVELS)]

        def mix_loop(i, inner):
            base = pl.multiple_of(i * 16, 16)
            pooled = [[], [], []]
            for e in range(2):
                rows = pl.ds(base + 8 * e, 8)
                acc = [None] * LATENT
                for l in range(LEVELS):
                    v = vals_ref[l, rows, :]
                    for q in range(LATENT):
                        term = parts[l][q] * v
                        acc[q] = term if acc[q] is None else acc[q] + term
                for q in range(LATENT):
                    pooled[q].append(acc[q])
            for q in range(LATENT):
                pooled_ref[pl.ds(base, 16), q * 128 : (q + 1) * 128] = jnp.concatenate(pooled[q], axis=0).astype(BF)
            return inner

        lax.fori_loop(0, D // 16, mix_loop, 0)
        latent = dot(pooled_ref[...], woutp_ref[...], 0, 0).astype(BF).astype(F32)
        normed = normalise(latent, gain)
        kv = dot(normed, wqkv_ref[:, D:]).astype(BF)

        @pl.when(group < 2)
        def _():
            first = group * 3
            for q in range(LATENT):
                kv_ref[first, 48 + 48 * q : 96 + 48 * q, :] = kv[q * 128 : q * 128 + 48]
                kv_ref[first + 1, 96 + 32 * q : 128 + 32 * q, :] = kv[q * 128 + 48 : q * 128 + 80]
                kv_ref[first + 2, 48 + 48 * q : 96 + 48 * q, :] = kv[q * 128 + 80 : q * 128 + 128]

        @pl.when(group >= 2)
        def _():
            first = 6 + (group - 2) * 6
            for half in range(2):
                for q in range(LATENT):
                    row = q * 128 + half * 64
                    kv_ref[first + 3 * half, 96 + 32 * q : 128 + 32 * q, :] = kv[row : row + 32]
                    kv_ref[first + 3 * half + 2, 96 + 32 * q : 128 + 32 * q, :] = kv[row + 32 : row + 64]
        return carry

    lax.fori_loop(0, 4, halo, 0)

    def project(rows, column):
        normed = normalise(rows.astype(F32), gain)
        normed = dot(permutation(384, 0), normed).astype(BF)
        q_ref[column] = (dot(normed, wqkv_ref[:, :D]).astype(BF).astype(F32) * (1.0 / math.sqrt(HD))).astype(BF)
        return dot(normed, wqkv_ref[:, D:]).astype(BF)

    rows = jnp.concatenate([latent_ref[28:32].reshape(192, D), latent_ref[0:4].reshape(192, D)], axis=0)
    kv = project(rows, 0)
    for side in range(2):
        first = 3 * (1 - side)
        kv_ref[first, 0:48, :] = kv[48 * side : 48 * side + 48]
        kv_ref[first + 1, 0:96, :] = kv[96 + 96 * side : 192 + 96 * side]
        kv_ref[first + 2, 0:48, :] = kv[288 + 48 * side : 336 + 48 * side]

    def own(column, carry):
        rows = latent_ref[pl.ds(8 * column - 4, 8)].reshape(384, D)
        kv = project(rows, column)
        first = 3 + 3 * column
        kv_ref[first, 0:96, :] = kv[0:96]
        kv_ref[first + 1, 0:192, :] = kv[96:288]
        kv_ref[first + 2, 0:96, :] = kv[288:384]
        return carry

    lax.fori_loop(1, 4, own, 0)

    key = lax.broadcasted_iota(jnp.int32, (1, 192), 1)
    odd_lane = lax.broadcasted_iota(jnp.int32, (1, 128), 1) >= HD

    def attend(column, window, row0, count, valid):
        for pair in range(HEADS // 2):
            lanes = slice(pair * 128, pair * 128 + 128)
            q = q_ref[column, row0 : row0 + count, lanes]
            nil = jnp.zeros_like(q)
            q2 = jnp.concatenate([jnp.where(odd_lane, nil, q), jnp.where(odd_lane, q, nil)], axis=0)
            expo = jnp.exp(dot(q2, kv_ref[window, :, lanes], 1, 1))
            if valid is not None:
                expo = jnp.where(valid, expo, 0.0)
            probs = (expo * (1.0 / jnp.sum(expo, axis=-1, keepdims=True))).astype(BF)
            both = dot(probs, kv_ref[window, :, D + pair * 128 : D + pair * 128 + 128])
            att_ref[row0 : row0 + count, lanes] = jnp.where(odd_lane, both[count:], both[:count]).astype(BF)

    inside = (edge_ref[0] == 0, edge_ref[1] == 0)
    plain = [(key < 96) | ok for ok in inside]
    corner = [(key < 48) | (key % 48 < 16) | ok for ok in inside]

    def finish(rows):
        natural = dot(permutation(384, 1), att_ref[...]).astype(BF)
        return (rows.astype(F32) + dot(natural, wproj_ref[...])).astype(BF)

    for side in range(2):
        first = 3 * (1 - side)
        attend(0, first, 48 * side, 48, corner[0])
        attend(0, first + 1, 96 + 96 * side, 96, None)
        attend(0, first + 2, 288 + 48 * side, 48, corner[1])
    done = finish(rows)
    out_ref[28:32] = done[:192].reshape(4, 3, 16, D)
    out_ref[0:4] = done[192:].reshape(4, 3, 16, D)

    def column_loop(column, carry):
        first = 3 + 3 * column
        attend(column, first, 0, 96, plain[0])
        attend(column, first + 1, 96, 192, None)
        attend(column, first + 2, 288, 96, plain[1])
        rows = latent_ref[pl.ds(8 * column - 4, 8)].reshape(384, D)
        out_ref[pl.ds(8 * column - 4, 8)] = finish(rows).reshape(8, 3, 16, D)
        return carry

    lax.fori_loop(1, 4, column_loop, 0)


def place(lev, tile):
    return {"lev": lev, "tile": tile}


def sum_kernel(terms_ref, total_ref, part_ref, band_ref, full_ref, send_sem, recv_sem):
    lev, tile = lax.axis_index("lev"), lax.axis_index("tile")
    bands, tiles = lax.axis_size("lev"), lax.axis_size("tile")
    barrier = pltpu.get_barrier_semaphore()
    for off in range(1, tiles):
        pl.semaphore_signal(barrier, inc=1, device_id=place(lev, lax.rem(tile + off, tiles)), device_id_type=pl.DeviceIdType.MESH)
    for off in range(1, bands):
        pl.semaphore_signal(barrier, inc=1, device_id=place(lax.rem(lev + off, bands), tile), device_id_type=pl.DeviceIdType.MESH)
    pl.semaphore_wait(barrier, tiles + bands - 2)

    def copy(src, dst, slot, device):
        return pltpu.make_async_remote_copy(src_ref=src, dst_ref=dst, send_sem=send_sem.at[slot], recv_sem=recv_sem.at[slot], device_id=device, device_id_type=pl.DeviceIdType.MESH)

    first = []
    for off in range(1, tiles):
        peer = lax.rem(tile + off, tiles)
        first.append(copy(terms_ref.at[peer], part_ref.at[off], off - 1, place(lev, peer)))
    for c in first:
        c.start()
    total = terms_ref[tile].astype(F32)
    for off, c in enumerate(first):
        c.wait_recv()
        total = total + part_ref[off + 1].astype(F32)
    band_ref[lev] = total.astype(BF)
    second = []
    for off in range(1, bands):
        second.append(copy(band_ref.at[lev], band_ref.at[lev], 14 + off, place(lax.rem(lev + off, bands), tile)))
    for c in second:
        c.start()
    for c in second:
        c.wait_recv()
    total = band_ref[0].astype(F32)
    for b in range(1, bands):
        total = total + band_ref[b].astype(F32)
    full_ref[tile] = total.astype(BF)
    third = []
    for off in range(1, tiles):
        third.append(copy(full_ref.at[tile], full_ref.at[tile], 21 + off, place(lev, lax.rem(tile + off, tiles))))
    for c in third:
        c.start()
    for c in third:
        c.wait_recv()
    total_ref[...] = full_ref[...]
    for c in first + second + third:
        c.wait_send()


def grads_kernel(total_ref, we_ref, queries_ref, wkv_ref, gembed_ref, gkv_ref, gout_ref, factor):
    qm = query_rows(queries_ref[...].astype(F32)).astype(BF)
    for j in range(4):
        gout_ref[:, j * 128 : (j + 1) * 128] = total_ref[j * D : (j + 1) * D, :].astype(F32) * factor
    values = total_ref[4 * D : 5 * D, :]
    keys = dot(qm, total_ref[5 * D : 5 * D + 32, :][:24], 0, 0)
    khigh, klow = split(keys)
    we = we_ref[...]
    gkv_ref[:, :D] = (dot(we, khigh, 0, 1) + dot(we, klow, 0, 1)) * factor
    gkv_ref[:, D:] = dot(we, values, 0, 1) * factor
    wk, wv = wkv_ref[:, :D], wkv_ref[:, D:]
    grad = dot(khigh, wk, 0, 1) + dot(klow, wk, 0, 1) + dot(values, wv, 0, 1)
    gembed_ref[...] = grad[:F] * factor


def whole(shape, dtype):
    return jax.ShapeDtypeStruct(shape, dtype)


def params(**kw):
    return pltpu.CompilerParams(vmem_limit_bytes=VMEM_LIMIT, **kw)


def halo_positions(ext):
    bands = ext.reshape(F, 40, 17, 8)
    low, mid, high = (bands[:, :, wa : wa + 15 : 2] for wa in range(3))

    def flat(block):
        return block.transpose(2, 0, 1, 3).reshape(LEVELS, F, -1)

    pieces = []
    for far, near in ((slice(0, 4), slice(4, 8)), (slice(36, 40), slice(32, 36))):
        pieces += [flat(low[:, far, :, 4:]), flat(low[:, far, :, :4]), flat(low[:, near, :, :4])]
        pieces += [flat(mid[:, far])]
        pieces += [flat(high[:, far, :, :4]), flat(high[:, far, :, 4:]), flat(high[:, near, :, 4:])]
    for c in (1, 2, 3):
        pieces += [flat(low[:, 8 * c : 8 * c + 8, :, :4]), flat(high[:, 8 * c : 8 * c + 8, :, 4:])]
    pieces.append(jnp.zeros((LEVELS, F, 64), ext.dtype))
    return jnp.concatenate(pieces, axis=2)


def per_device(inputs, level_ids, level_table, w_embed, queries, w_kv, w_out, gain, w_qkv, w_proj, d_latent):
    band = lax.axis_index("lev")
    bands = lax.axis_size("lev")
    tiles = lax.axis_size("tile")
    lon_rows, lat_rows = d_latent.shape[:2]
    x = inputs[0]
    ring = [(i, (i + 1) % tiles) for i in range(tiles)]
    back = [(target, source) for source, target in ring]
    west = lax.ppermute(x[:, 28:32], "tile", ring)
    east = lax.ppermute(x[:, 0:4], "tile", back)
    own = x.reshape(F, 32, 8, 16).transpose(2, 0, 1, 3).reshape(LEVELS, F, 512)
    own = lax.all_to_all(own, "lev", split_axis=0, concat_axis=0, tiled=True)
    ext = jnp.pad(jnp.concatenate([west, x, east], axis=1), ((0, 0), (0, 0), (4, 4)))
    far = lax.all_to_all(halo_positions(ext), "lev", split_axis=0, concat_axis=0, tiled=True)

    onehot = (level_ids[:, None] == jnp.arange(level_table.shape[0], dtype=jnp.int32)[None, :]).astype(BF)
    rows = jnp.dot(onehot, level_table, preferred_element_type=F32).astype(BF)
    we = jnp.concatenate([w_embed, rows, jnp.zeros((KX - F - LEVELS, D), BF)], axis=0)
    w2, woutp = pl.pallas_call(
        weights_kernel,
        out_shape=(whole((MV, 2 * KX), BF), whole((D, D), BF)),
        compiler_params=params(),
        name="weights",
    )(we, queries, w_kv, w_out)

    d_nat = d_latent.transpose(0, 2, 1, 3)
    block = pl.BlockSpec((8, LATENT, 16, D), lambda g: (g, 0, 0, 0))

    def fixed(shape):
        return pl.BlockSpec(shape, lambda g: (0,) * len(shape))

    latent, terms = pl.pallas_call(
        pool_kernel,
        grid=(4,),
        in_specs=[
            pl.BlockSpec((LEVELS, F, 128), lambda g: (0, 0, g)),
            block,
            fixed((MV, 2 * KX)),
            fixed((D, D)),
        ],
        out_specs=[block, fixed((TERMS, KX))],
        out_shape=(whole(d_nat.shape, BF), whole((TERMS, KX), BF)),
        scratch_shapes=[
            pltpu.VMEM((LEVELS, D, 128), F32),
            pltpu.VMEM((D, 384), F32),
            pltpu.VMEM((D, 384), BF),
            pltpu.VMEM((LEVELS // 2, MV, 256), BF),
            pltpu.VMEM((MV, KX), F32),
            pltpu.VMEM((4 * D, 128), F32),
        ],
        compiler_params=params(dimension_semantics=("arbitrary",)),
        name="pool",
    )(own, d_nat, w2, woutp)

    factor = 1.0 / math.sqrt(lon_rows * lat_rows * bands * tiles)
    total = pl.pallas_call(
        sum_kernel,
        in_specs=[pl.BlockSpec(memory_space=pltpu.VMEM)],
        out_specs=pl.BlockSpec(memory_space=pltpu.VMEM),
        out_shape=whole((16, CHUNK, KX), BF),
        scratch_shapes=[
            pltpu.VMEM((16, CHUNK, KX), BF),
            pltpu.VMEM((8, CHUNK, KX), BF),
            pltpu.VMEM((16, CHUNK, KX), BF),
            pltpu.SemaphoreType.DMA((37,)),
            pltpu.SemaphoreType.DMA((37,)),
        ],
        compiler_params=params(collective_id=1, has_side_effects=True),
        name="sums",
    )(terms.reshape(16, CHUNK, KX))

    edge = jnp.stack([band == 0, band == bands - 1]).astype(jnp.int32)
    vmem = pl.BlockSpec(memory_space=pltpu.VMEM)
    out = pl.pallas_call(
        window_kernel,
        in_specs=[pl.BlockSpec(memory_space=pltpu.SMEM)] + [vmem] * 7,
        out_specs=vmem,
        out_shape=whole(d_nat.shape, BF),
        scratch_shapes=[
            pltpu.VMEM((LEVELS, D, 128), F32),
            pltpu.VMEM((D, 384), BF),
            pltpu.VMEM((4, 384, D), BF),
            pltpu.VMEM((18, 192, 2 * D), BF),
            pltpu.VMEM((384, D), BF),
        ],
        compiler_params=params(),
        name="windows",
    )(edge, far, latent, w2, woutp, gain.reshape(1, D), w_qkv, w_proj)

    gembed, gkv, gout = pl.pallas_call(
        functools.partial(grads_kernel, factor=factor),
        out_shape=(whole((F, D), F32), whole((D, 2 * D), F32), whole((D, D), F32)),
        compiler_params=params(),
        name="grads",
    )(total.reshape(TERMS, KX), we, queries, w_kv)
    return (out.transpose(0, 2, 1, 3), gembed, gkv, gout)


def solution(mesh):
    placed = (P("lev", None, "tile", None),) + (P(),) * 9 + (P("tile", "lev", None, None),)
    return jax.shard_map(
        per_device,
        mesh=mesh,
        in_specs=placed,
        out_specs=(P("tile", "lev", None, None), P(), P(), P()),
        check_vma=False,
    )
```

profile of v0, /device:TPU:1, one launch (start us, length us, event | category | flops | bytes accessed | tf_op | source)
XLA Modules:
  0.0 124.0 jit_solution(16228705444164482162)
XLA Ops:
  0.6 0.0 copy-start
  0.6 1.7 %copy.19 = bf16[1,80,32,128]{1,3,2,0:T(8,128)(2,1)S(1)} copy(bf16[1,80,32,128]{3,2,1,0:T(8,128)(2,1)} %param.11) | data formatting | bytes 1310720 | tf_op args[0]
  2.4 4.4 %collective-permute-start = (bf16[80,4,128]{0,2,1:T(8,128)(2,1)S(1)}, bf16[80,4,128]{0,2,1:T(8,128)(2,1)S(1)}, u32[]{:S(2)}, u32[]{:S(2)}) collective-permute-start(bf16[80,4,128]{0,2,1:T(8,128)(2,1)S(1)} %get-tuple-element.21), channel_id=1, source_target_pairs={{0,1},{1,2},{2,3},{3,4},{4,5},{5,6},{6,7},{7,8},{8,9},{9,10},{10,1... | collective-permute-start | bytes 245768 | tf_op jit(solution)/shard_map/ppermute | solution.py:416
  6.8 0.0 collective-permute-start.1
  6.8 0.2 copy.61
  6.9 1.2 copy.62
  8.2 4.1 %all-to-all-start.1 = ((bf16[8,80,512]{2,1,0:T(8,128)(2,1)}), bf16[8,80,512]{2,1,0:T(8,128)(2,1)S(1)}, u32[]{:S(2)}, u32[]{:S(2)}) async-start(bf16[8,80,512]{2,1,0:T(8,128)(2,1)} %copy.62), calls=%async_computation.1 | async-start | bytes 1310720 | tf_op jit(solution)/shard_map/all_to_all | solution.py:419
  12.3 0.0 collective-permute-done
  12.3 0.3 collective-permute-done.1
  12.6 0.5 fusion.6
  13.1 0.3 fusion.8
  13.5 0.1 copy.50
  13.6 0.1 copy.43
  13.8 0.2 slice_bitcast_fusion.8
  14.0 0.2 slice_bitcast_fusion
  14.2 0.6 copy.26
  15.0 0.1 copy.58
  15.2 0.2 copy.56
  15.3 0.2 copy.54
  15.5 0.2 copy.55
  15.6 0.2 copy.57
  15.8 0.2 copy.59
  15.9 0.1 copy.49
  16.1 0.1 copy.48
  16.2 0.1 copy.47
  16.4 0.1 copy.42
  16.5 0.1 copy.41
  16.7 0.1 copy.40
  16.8 0.1 copy.44
  17.0 0.1 copy.45
  17.1 0.9 copy.46
  18.0 0.8 copy.51
  18.8 0.8 copy.52
  19.6 0.8 copy.53
  20.4 0.7 broadcast_in_dim.8
  21.1 3.7 %concatenate.10 = bf16[8,80,512]{2,1,0:T(8,128)(2,1)} concatenate(bf16[8,80,16]{2,1,0:T(8,128)(2,1)S(1)} %copy.40, bf16[8,80,16]{2,1,0:T(8,128)(2,1)S(1)} %copy.41, bf16[8,80,16]{2,1,0:T(8,128)(2,1)S(1)} %copy.42, bf16[8,80,32]{2,1,0:T(8,128)(2,1)S(1)} %copy.43, bf16[8,80,16]{2,1,0:T(8,128)(2,1)S(1)} %copy.44, bf16[8,80,16]{2,1,0:T(8,128)(2,1)S(1)} %copy.45, ...), dimensions={2} | concatenate | bytes 1310720 | tf_op jit(solution)/shard_map/concatenate | solution.py:405
  24.8 0.0 all-to-all-done.1.x_ref
  24.8 4.8 %all-to-all-start = ((bf16[8,80,512]{2,1,0:T(8,128)(2,1)}), bf16[8,80,512]{2,1,0:T(8,128)(2,1)S(1)}, u32[]{:S(2)}, u32[]{:S(2)}) async-start(bf16[8,80,512]{2,1,0:T(8,128)(2,1)} %concatenate.10), calls=%async_computation | async-start | bytes 1310720 | tf_op jit(solution)/shard_map/all_to_all | solution.py:421
  29.6 0.1 pad.7.clone
  29.7 0.2 convolution_convert_fusion
  29.9 0.8 maximum_maximum_fusion.we_ref
  30.7 3.4 %weights.1 = (bf16[544,256]{1,0:T(8,128)(2,1)}, bf16[512,512]{1,0:T(8,128)(2,1)}) custom-call(bf16[128,512]{1,0:T(8,128)(2,1)} %maximum_maximum_fusion.we_ref, bf16[3,512]{1,0:T(4,128)(2,1)} %queries_ref.3, bf16[512,1024]{1,0:T(8,128)(2,1)} %wkv_ref.3, bf16[512,512]{1,0:T(8,128)(2,1)} %wout_ref.1), custom_call_target="tpu_custom_call" | custom-call | tf_op jit(solution)/shard_map/weights/pallas_call | solution.py:426
  34.1 0.6 add_convert_fusion.edge_ref
  34.7 15.9 %pool.1 = (bf16[32,3,16,512]{3,2,1,0:T(8,128)(2,1)}, bf16[2816,128]{1,0:T(8,128)(2,1)}) custom-call(bf16[8,80,512]{2,1,0:T(8,128)(2,1)} %copy-done.2, bf16[32,3,16,512]{3,2,1,0:T(8,128)(2,1)} %bitcast.82, bf16[544,256]{1,0:T(8,128)(2,1)} %get-tuple-element.11.w2_ref, bf16[512,512]{1,0:T(8,128)(2,1)} %get-tuple-element.12.woutp_ref), custom_call_target="tpu_custom_call" | custom-call | tf_op jit(solution)/shard_map/pool/pallas_call | solution.py:439
  50.5 39.9 %sums.1 = bf16[16,176,128]{2,1,0:T(8,128)(2,1)} custom-call(bf16[16,176,128]{2,1,0:T(8,128)(2,1)} %bitcast.84), custom_call_target="tpu_custom_call" | custom-call | tf_op jit(solution)/shard_map/sums/pallas_call | solution.py:463
  90.4 4.1 %grads.1 = (f32[80,512]{1,0:T(8,128)}, f32[512,1024]{1,0:T(8,128)}, f32[512,512]{1,0:T(8,128)}) custom-call(bf16[2816,128]{1,0:T(8,128)(2,1)} %bitcast.81, bf16[128,512]{1,0:T(8,128)(2,1)} %maximum_maximum_fusion.we_ref, bf16[3,512]{1,0:T(4,128)(2,1)} %queries_ref.3, bf16[512,1024]{1,0:T(8,128)(2,1)} %wkv_ref.3), custom_call_target="tpu_custom_call" | custom-call | tf_op jit(solution)/shard_map/grads/pallas_call | solution.py:497
  94.5 0.8 copy-done.1
  95.3 28.7 %windows.1 = bf16[32,3,16,512]{3,2,1,0:T(8,128)(2,1)} custom-call(s32[2]{0:T(128)} %add_convert_fusion.edge_ref, bf16[8,80,512]{2,1,0:T(8,128)(2,1)} %copy-done.1, bf16[32,3,16,512]{3,2,1,0:T(8,128)(2,1)} %get-tuple-element.13.latent_ref, bf16[544,256]{1,0:T(8,128)(2,1)} %get-tuple-element.11.w2_ref, bf16[512,512]{1,0:T(8,128)(2,1)} %get-tuple-element.12.woutp_ref, ...), custom_call_target="tpu_custom_call" | custom-call | tf_op jit(solution)/shard_map/windows/pallas_call | solution.py:481
  (30 shorter events, 0.2 us)
Async XLA Ops:
  0.6 29.1 %copy-start = (bf16[13,512]{1,0:T(8,128)(2,1)S(1)}, bf16[13,512]{1,0:T(8,128)(2,1)}, u32[]{:S(2)}) copy-start(bf16[13,512]{1,0:T(8,128)(2,1)} %param.13) | copy-start | bytes 39940
  2.4 9.9 %collective-permute-start = (bf16[80,4,128]{0,2,1:T(8,128)(2,1)S(1)}, bf16[80,4,128]{0,2,1:T(8,128)(2,1)S(1)}, u32[]{:S(2)}, u32[]{:S(2)}) collective-permute-start(bf16[80,4,128]{0,2,1:T(8,128)(2,1)S(1)} %get-tuple-element.21), channel_id=1, source_target_pairs={{0,1},{1,2},{2,3},{3,4},{4,5},{5,6},{6,7},{7,8},{8,9},{9,10},{10,1... | collective-permute-start | bytes 245768 | tf_op jit(solution)/shard_map/ppermute | solution.py:416
  6.8 5.9 %collective-permute-start.1 = (bf16[80,4,128]{0,2,1:T(8,128)(2,1)S(1)}, bf16[80,4,128]{0,2,1:T(8,128)(2,1)S(1)}, u32[]{:S(2)}, u32[]{:S(2)}) collective-permute-start(bf16[80,4,128]{0,2,1:T(8,128)(2,1)S(1)} %get-tuple-element.22), channel_id=1, source_target_pairs={{1,0},{2,1},{3,2},{4,3},{5,4},{6,5},{7,6},{8,7},{9,8},{10,9},{11,1... | collective-permute-start | bytes 245768 | tf_op jit(solution)/shard_map/ppermute | solution.py:417
  8.2 16.6 %all-to-all-start.1 = ((bf16[8,80,512]{2,1,0:T(8,128)(2,1)}), bf16[8,80,512]{2,1,0:T(8,128)(2,1)S(1)}, u32[]{:S(2)}, u32[]{:S(2)}) async-start(bf16[8,80,512]{2,1,0:T(8,128)(2,1)} %copy.62), calls=%async_computation.1 | async-start | bytes 1310720 | tf_op jit(solution)/shard_map/all_to_all | solution.py:419
  21.1 8.6 %copy-start.4 = (s32[8]{0:T(128)S(1)}, s32[8]{0:T(128)}, u32[]{:S(2)}) copy-start(s32[8]{0:T(128)} %param.12) | copy-start | bytes 100
  21.1 8.8 %copy-start.3 = (bf16[80,512]{1,0:T(8,128)(2,1)S(1)}, bf16[80,512]{1,0:T(8,128)(2,1)}, u32[]{:S(2)}) copy-start(bf16[80,512]{1,0:T(8,128)(2,1)} %param.14) | copy-start | bytes 245764
  24.8 9.3 %copy-start.2 = (bf16[8,80,512]{2,1,0:T(8,128)(2,1)}, bf16[8,80,512]{2,1,0:T(8,128)(2,1)S(1)}, u32[]{:S(2)}) copy-start(bf16[8,80,512]{2,1,0:T(8,128)(2,1)S(1)} %all-to-all-done.1.x_ref) | copy-start | bytes 1966084
  24.8 69.7 %all-to-all-start = ((bf16[8,80,512]{2,1,0:T(8,128)(2,1)}), bf16[8,80,512]{2,1,0:T(8,128)(2,1)S(1)}, u32[]{:S(2)}, u32[]{:S(2)}) async-start(bf16[8,80,512]{2,1,0:T(8,128)(2,1)} %concatenate.10), calls=%async_computation | async-start | bytes 1310720 | tf_op jit(solution)/shard_map/all_to_all | solution.py:421
  94.5 0.8 copy-start.1
where the time goes:
time: 125 us; the launch traced here: 124 us
  Pallas kernels  91.9 us (74%)
  local copies, waits for them, and re-layouts  15.5 us (12%)
  starting transfers between devices  13.3 us (11%)
  other arithmetic  1.79 us (1%)
    pallas_call x1, Pallas kernels, per_device(): pl.pallas_call(sum_kernel, in_specs=[pl.BlockSpec(memory_space=pltpu.VMEM...  39.9 us
    pallas_call x1, Pallas kernels, per_device(): pl.pallas_call(window_kernel, in_specs=[pl.BlockSpec(memory_space=pltpu.S...  28.7 us
    pallas_call x1, Pallas kernels, per_device(): pl.pallas_call(pool_kernel, grid=(4,), in_specs=[pl.BlockSpec((LEVELS, F,...  15.9 us
    reshape x21, local copies, waits for them, and re-layouts, flat(): return block.transpose(2, 0, 1, 3).reshape(LEVELS, F, -1)  5.63 us
    all_to_all x1, starting transfers between devices, per_device(): lax.all_to_all(halo_positions(ext), 'lev', split_axis=0, concat_axis=0, t...  4.82 us
    ppermute x1, starting transfers between devices, per_device(): west = lax.ppermute(x[:, 28:32], 'tile', ring)  4.37 us
    all_to_all x1, starting transfers between devices, per_device(): own = lax.all_to_all(own, 'lev', split_axis=0, concat_axis=0, tiled=True)  4.13 us
    pallas_call x1, Pallas kernels, per_device(): pl.pallas_call(functools.partial(grads_kernel, factor=factor), out_shape=...  4.07 us
  transfers between devices with their start and end apart: 4, of which 1 were waited for; matrix products, arithmetic and copies ran while one was open for 12% of the time, Pallas kernels for 51%

commit v1 on v0

--- a/solution.py
+++ b/solution.py
@@ -193,8 +193,64 @@
     return jnp.where(src == want, 1.0, 0.0).astype(BF)
 
 
-def window_kernel(edge_ref, xh_ref, latent_ref, w2_ref, woutp_ref, gain_ref, wqkv_ref, wproj_ref, out_ref, vals_ref, pooled_ref, q_ref, kv_ref, att_ref):
+def place(lev, tile):
+    return {"lev": lev, "tile": tile}
+
+
+def sum_stages(terms_ref, part_ref, band_ref, full_ref, send_sem, recv_sem):
+    lev, tile = lax.axis_index("lev"), lax.axis_index("tile")
+    bands, tiles = lax.axis_size("lev"), lax.axis_size("tile")
+
+    def copy(src, dst, slot, device):
+        return pltpu.make_async_remote_copy(src_ref=src, dst_ref=dst, send_sem=send_sem.at[slot], recv_sem=recv_sem.at[slot], device_id=device, device_id_type=pl.DeviceIdType.MESH)
+
+    tile_peers = [place(lev, lax.rem(tile + off, tiles)) for off in range(1, tiles)]
+    lev_peers = [place(lax.rem(lev + off, bands), tile) for off in range(1, bands)]
+    first = [copy(terms_ref.at[peer["tile"]], part_ref.at[i], i, peer) for i, peer in enumerate(tile_peers)]
+    second = [copy(band_ref.at[lev], band_ref.at[lev], 15 + i, peer) for i, peer in enumerate(lev_peers)]
+    third = [copy(full_ref.at[tile], full_ref.at[tile], 22 + i, peer) for i, peer in enumerate(tile_peers)]
+
+    def greet():
+        barrier = pltpu.get_barrier_semaphore()
+        for peer in tile_peers + lev_peers:
+            pl.semaphore_signal(barrier, inc=1, device_id=peer, device_id_type=pl.DeviceIdType.MESH)
+        pl.semaphore_wait(barrier, tiles + bands - 2)
+        for c in first:
+            c.start()
+
+    def over_lev():
+        total = terms_ref[tile].astype(F32)
+        for i, c in enumerate(first):
+            c.wait_recv()
+            total = total + part_ref[i].astype(F32)
+        band_ref[lev] = total.astype(BF)
+        for c in second:
+            c.start()
+
+    def gather():
+        for c in second:
+            c.wait_recv()
+        total = band_ref[0].astype(F32)
+        for b in range(1, bands):
+            total = total + band_ref[b].astype(F32)
+        full_ref[tile] = total.astype(BF)
+        for c in third:
+            c.start()
+
+    def close(total_ref):
+        for c in third:
+            c.wait_recv()
+        total_ref[...] = full_ref[...]
+        for c in first + second + third:
+            c.wait_send()
+
+    return greet, over_lev, gather, close
+
+
+def window_kernel(terms_ref, edge_ref, xh_ref, latent_ref, w2_ref, woutp_ref, gain_ref, wqkv_ref, att_ref, total_ref, vals_ref, pooled_ref, q_ref, kv_ref, part_ref, band_ref, full_ref, send_sem, recv_sem):
     gain = gain_ref[...]
+    greet, over_lev, gather, close = sum_stages(terms_ref, part_ref, band_ref, full_ref, send_sem, recv_sem)
+    greet()
 
     def halo(group, carry):
         lane0 = pl.multiple_of(group * 128, 128)
@@ -267,6 +323,7 @@
         return carry
 
     lax.fori_loop(1, 4, own, 0)
+    over_lev()
 
     key = lax.broadcasted_iota(jnp.int32, (1, 192), 1)
     odd_lane = lax.broadcasted_iota(jnp.int32, (1, 128), 1) >= HD
@@ -282,89 +339,52 @@
                 expo = jnp.where(valid, expo, 0.0)
             probs = (expo * (1.0 / jnp.sum(expo, axis=-1, keepdims=True))).astype(BF)
             both = dot(probs, kv_ref[window, :, D + pair * 128 : D + pair * 128 + 128])
-            att_ref[row0 : row0 + count, lanes] = jnp.where(odd_lane, both[count:], both[:count]).astype(BF)
+            att_ref[column, row0 : row0 + count, lanes] = jnp.where(odd_lane, both[count:], both[:count]).astype(BF)
 
     inside = (edge_ref[0] == 0, edge_ref[1] == 0)
     plain = [(key < 96) | ok for ok in inside]
     corner = [(key < 48) | (key % 48 < 16) | ok for ok in inside]
-
-    def finish(rows):
-        natural = dot(permutation(384, 1), att_ref[...]).astype(BF)
-        return (rows.astype(F32) + dot(natural, wproj_ref[...])).astype(BF)
 
     for side in range(2):
         first = 3 * (1 - side)
         attend(0, first, 48 * side, 48, corner[0])
         attend(0, first + 1, 96 + 96 * side, 96, None)
         attend(0, first + 2, 288 + 48 * side, 48, corner[1])
-    done = finish(rows)
-    out_ref[28:32] = done[:192].reshape(4, 3, 16, D)
-    out_ref[0:4] = done[192:].reshape(4, 3, 16, D)
+    gather()
 
     def column_loop(column, carry):
         first = 3 + 3 * column
         attend(column, first, 0, 96, plain[0])
         attend(column, first + 1, 96, 192, None)
         attend(column, first + 2, 288, 96, plain[1])
+        return carry
+
+    lax.fori_loop(1, 4, column_loop, 0)
+    close(total_ref)
+
+
+def finish_kernel(att_ref, latent_ref, wproj_ref, total_ref, we_ref, queries_ref, wkv_ref, out_ref, gembed_ref, gkv_ref, gout_ref, factor):
+    back = permutation(384, 1)
+
+    def finish(column, rows):
+        natural = dot(back, att_ref[column]).astype(BF)
+        return (rows.astype(F32) + dot(natural, wproj_ref[...])).astype(BF)
+
+    rows = jnp.concatenate([latent_ref[28:32].reshape(192, D), latent_ref[0:4].reshape(192, D)], axis=0)
+    done = finish(0, rows)
+    out_ref[28:32] = done[:192].reshape(4, 3, 16, D)
+    out_ref[0:4] = done[192:].reshape(4, 3, 16, D)
+
+    def column_loop(column, carry):
         rows = latent_ref[pl.ds(8 * column - 4, 8)].reshape(384, D)
-        out_ref[pl.ds(8 * column - 4, 8)] = finish(rows).reshape(8, 3, 16, D)
+        out_ref[pl.ds(8 * column - 4, 8)] = finish(column, rows).reshape(8, 3, 16, D)
         return carry
 
     lax.fori_loop(1, 4, column_loop, 0)
-
-
-def place(lev, tile):
-    return {"lev": lev, "tile": tile}
-
-
-def sum_kernel(terms_ref, total_ref, part_ref, band_ref, full_ref, send_sem, recv_sem):
-    lev, tile = lax.axis_index("lev"), lax.axis_index("tile")
-    bands, tiles = lax.axis_size("lev"), lax.axis_size("tile")
-    barrier = pltpu.get_barrier_semaphore()
-    for off in range(1, tiles):
-        pl.semaphore_signal(barrier, inc=1, device_id=place(lev, lax.rem(tile + off, tiles)), device_id_type=pl.DeviceIdType.MESH)
-    for off in range(1, bands):
-        pl.semaphore_signal(barrier, inc=1, device_id=place(lax.rem(lev + off, bands), tile), device_id_type=pl.DeviceIdType.MESH)
-    pl.semaphore_wait(barrier, tiles + bands - 2)
-
-    def copy(src, dst, slot, device):
-        return pltpu.make_async_remote_copy(src_ref=src, dst_ref=dst, send_sem=send_sem.at[slot], recv_sem=recv_sem.at[slot], device_id=device, device_id_type=pl.DeviceIdType.MESH)
-
-    first = []
-    for off in range(1, tiles):
-        peer = lax.rem(tile + off, tiles)
-        first.append(copy(terms_ref.at[peer], part_ref.at[off], off - 1, place(lev, peer)))
-    for c in first:
-        c.start()
-    total = terms_ref[tile].astype(F32)
-    for off, c in enumerate(first):
-        c.wait_recv()
-        total = total + part_ref[off + 1].astype(F32)
-    band_ref[lev] = total.astype(BF)
-    second = []
-    for off in range(1, bands):
-        second.append(copy(band_ref.at[lev], band_ref.at[lev], 14 + off, place(lax.rem(lev + off, bands), tile)))
-    for c in second:
-        c.start()
-    for c in second:
-        c.wait_recv()
-    total = band_ref[0].astype(F32)
-    for b in range(1, bands):
-        total = total + band_ref[b].astype(F32)
-    full_ref[tile] = total.astype(BF)
-    third = []
-    for off in range(1, tiles):
-        third.append(copy(full_ref.at[tile], full_ref.at[tile], 21 + off, place(lev, lax.rem(tile + off, tiles))))
-    for c in third:
-        c.start()
-    for c in third:
-        c.wait_recv()
-    total_ref[...] = full_ref[...]
-    for c in first + second + third:
-        c.wait_send()
-
-
-def grads_kernel(total_ref, we_ref, queries_ref, wkv_ref, gembed_ref, gkv_ref, gout_ref, factor):
+    grads(total_ref, we_ref, queries_ref, wkv_ref, gembed_ref, gkv_ref, gout_ref, factor)
+
+
+def grads(total_ref, we_ref, queries_ref, wkv_ref, gembed_ref, gkv_ref, gout_ref, factor):
     qm = query_rows(queries_ref[...].astype(F32)).astype(BF)
     for j in range(4):
         gout_ref[:, j * 128 : (j + 1) * 128] = total_ref[j * D : (j + 1) * D, :].astype(F32) * factor
@@ -460,46 +480,34 @@
     )(own, d_nat, w2, woutp)
 
     factor = 1.0 / math.sqrt(lon_rows * lat_rows * bands * tiles)
-    total = pl.pallas_call(
-        sum_kernel,
-        in_specs=[pl.BlockSpec(memory_space=pltpu.VMEM)],
-        out_specs=pl.BlockSpec(memory_space=pltpu.VMEM),
-        out_shape=whole((16, CHUNK, KX), BF),
+    edge = jnp.stack([band == 0, band == bands - 1]).astype(jnp.int32)
+    vmem = pl.BlockSpec(memory_space=pltpu.VMEM)
+    att, total = pl.pallas_call(
+        window_kernel,
+        in_specs=[vmem, pl.BlockSpec(memory_space=pltpu.SMEM)] + [vmem] * 6,
+        out_specs=(vmem, vmem),
+        out_shape=(whole((4, 384, D), BF), whole((16, CHUNK, KX), BF)),
         scratch_shapes=[
-            pltpu.VMEM((16, CHUNK, KX), BF),
+            pltpu.VMEM((LEVELS, D, 128), F32),
+            pltpu.VMEM((D, 384), BF),
+            pltpu.VMEM((4, 384, D), BF),
+            pltpu.VMEM((18, 192, 2 * D), BF),
+            pltpu.VMEM((15, CHUNK, KX), BF),
             pltpu.VMEM((8, CHUNK, KX), BF),
             pltpu.VMEM((16, CHUNK, KX), BF),
             pltpu.SemaphoreType.DMA((37,)),
             pltpu.SemaphoreType.DMA((37,)),
         ],
         compiler_params=params(collective_id=1, has_side_effects=True),
-        name="sums",
-    )(terms.reshape(16, CHUNK, KX))
-
-    edge = jnp.stack([band == 0, band == bands - 1]).astype(jnp.int32)
-    vmem = pl.BlockSpec(memory_space=pltpu.VMEM)
-    out = pl.pallas_call(
-        window_kernel,
-        in_specs=[pl.BlockSpec(memory_space=pltpu.SMEM)] + [vmem] * 7,
-        out_specs=vmem,
-        out_shape=whole(d_nat.shape, BF),
-        scratch_shapes=[
-            pltpu.VMEM((LEVELS, D, 128), F32),
-            pltpu.VMEM((D, 384), BF),
-            pltpu.VMEM((4, 384, D), BF),
-            pltpu.VMEM((18, 192, 2 * D), BF),
-            pltpu.VMEM((384, D), BF),
-        ],
+        name="windows",
+    )(terms.reshape(16, CHUNK, KX), edge, far, latent, w2, woutp, gain.reshape(1, D), w_qkv)
+
+    out, gembed, gkv, gout = pl.pallas_call(
+        functools.partial(finish_kernel, factor=factor),
+        out_shape=(whole(d_nat.shape, BF), whole((F, D), F32), whole((D, 2 * D), F32), whole((D, D), F32)),
         compiler_params=params(),
-        name="windows",
-    )(edge, far, latent, w2, woutp, gain.reshape(1, D), w_qkv, w_proj)
-
-    gembed, gkv, gout = pl.pallas_call(
-        functools.partial(grads_kernel, factor=factor),
-        out_shape=(whole((F, D), F32), whole((D, 2 * D), F32), whole((D, D), F32)),
-        compiler_params=params(),
-        name="grads",
-    )(total.reshape(TERMS, KX), we, queries, w_kv)
+        name="finish",
+    )(att, latent, w_proj, total.reshape(TERMS, KX), we, queries, w_kv)
     return (out.transpose(0, 2, 1, 3), gembed, gkv, gout)
 
 

time: 125 us -> 105 us (0.84)
  Pallas kernels: 91.9 us -> 72.6 us
    pallas_call x3 -> x2, Pallas kernels: 72.6 us -> 53.3 us  [the longest x1 45.3 us: per_device(): pl.pallas_call(window_kernel, in_specs=[vmem, pl.BlockSpec(memory_space=p...]
  transfers between devices with their start and end apart: 4 -> 4, of which waited for: 1 -> 1; matrix products, arithmetic and copies ran while one was open for 12% -> 14% of each run, Pallas kernels for 51% -> 18%
where the time goes in v1:
time: 105 us
  Pallas kernels  72.6 us (69%)
  local copies, waits for them, and re-layouts  15.6 us (15%)
  starting transfers between devices  13.3 us (13%)
  other arithmetic  1.86 us (2%)
    pallas_call x1, Pallas kernels, per_device(): pl.pallas_call(window_kernel, in_specs=[vmem, pl.BlockSpec(memory_space=p...  45.3 us
    pallas_call x1, Pallas kernels, per_device(): pl.pallas_call(pool_kernel, grid=(4,), in_specs=[pl.BlockSpec((LEVELS, F,...  15.9 us
    pallas_call x1, Pallas kernels, per_device(): pl.pallas_call(functools.partial(finish_kernel, factor=factor), out_shape...  8.02 us
    reshape x21, local copies, waits for them, and re-layouts, flat(): return block.transpose(2, 0, 1, 3).reshape(LEVELS, F, -1)  5.64 us
    all_to_all x1, starting transfers between devices, per_device(): lax.all_to_all(halo_positions(ext), 'lev', split_axis=0, concat_axis=0, t...  4.82 us
    ppermute x1, starting transfers between devices, per_device(): west = lax.ppermute(x[:, 28:32], 'tile', ring)  4.37 us
    all_to_all x1, starting transfers between devices, per_device(): own = lax.all_to_all(own, 'lev', split_axis=0, concat_axis=0, tiled=True)  4.13 us
    concatenate x1, local copies, waits for them, and re-layouts, halo_positions(): return jnp.concatenate(pieces, axis=2)  3.69 us
  transfers between devices with their start and end apart: 4, of which 1 were waited for; matrix products, arithmetic and copies ran while one was open for 14% of the time, Pallas kernels for 18%

profile of v1, /device:TPU:1, one launch (start us, length us, event | category | flops | bytes accessed | tf_op | source)
XLA Modules:
  0.0 104.9 jit_solution(17536546102013393252)
XLA Ops:
  0.6 0.0 copy-start
  0.6 1.7 %copy.19 = bf16[1,80,32,128]{1,3,2,0:T(8,128)(2,1)S(1)} copy(bf16[1,80,32,128]{3,2,1,0:T(8,128)(2,1)} %param.11) | data formatting | bytes 1310720 | tf_op args[0]
  2.4 4.4 %collective-permute-start = (bf16[80,4,128]{0,2,1:T(8,128)(2,1)S(1)}, bf16[80,4,128]{0,2,1:T(8,128)(2,1)S(1)}, u32[]{:S(2)}, u32[]{:S(2)}) collective-permute-start(bf16[80,4,128]{0,2,1:T(8,128)(2,1)S(1)} %get-tuple-element.27), channel_id=1, source_target_pairs={{0,1},{1,2},{2,3},{3,4},{4,5},{5,6},{6,7},{7,8},{8,9},{9,10},{10,1... | collective-permute-start | bytes 245768 | tf_op jit(solution)/shard_map/ppermute | solution.py:436
  6.8 0.0 collective-permute-start.1
  6.8 0.2 copy.20
  6.9 1.2 %copy.21 = bf16[8,80,512]{2,1,0:T(8,128)(2,1)} copy(bf16[8,80,512]{1,2,0:T(8,128)(2,1)S(1)} %bitcast.80) | data formatting | bytes 1310720 | tf_op jit(solution)/shard_map/reshape | solution.py:438
  8.2 4.1 %all-to-all-start = ((bf16[8,80,512]{2,1,0:T(8,128)(2,1)}), bf16[8,80,512]{2,1,0:T(8,128)(2,1)S(1)}, u32[]{:S(2)}, u32[]{:S(2)}) async-start(bf16[8,80,512]{2,1,0:T(8,128)(2,1)} %copy.21), calls=%async_computation | async-start | bytes 1310720 | tf_op jit(solution)/shard_map/all_to_all | solution.py:439
  12.3 0.0 collective-permute-done
  12.3 0.3 collective-permute-done.1
  12.6 0.5 fusion.6
  13.1 0.4 fusion.8
  13.6 0.1 copy.53
  13.7 0.1 copy.46
  13.9 0.2 slice_bitcast_fusion.8
  14.1 0.2 slice_bitcast_fusion
  14.3 0.6 copy.29
  15.1 0.1 copy.61
  15.3 0.2 copy.59
  15.4 0.2 copy.57
  15.6 0.2 copy.58
  15.7 0.2 copy.60
  15.9 0.2 copy.62
  16.0 0.1 copy.52
  16.2 0.1 copy.51
  16.3 0.1 copy.50
  16.5 0.1 copy.45
  16.6 0.1 copy.44
  16.8 0.1 copy.43
  17.0 0.1 copy.47
  17.1 0.1 copy.48
  17.3 0.9 copy.49
  18.2 0.8 copy.54
  19.0 0.8 copy.55
  19.7 0.8 copy.56
  20.5 0.7 broadcast_in_dim.9
  21.2 3.7 %concatenate.11 = bf16[8,80,512]{2,1,0:T(8,128)(2,1)} concatenate(bf16[8,80,16]{2,1,0:T(8,128)(2,1)S(1)} %copy.43, bf16[8,80,16]{2,1,0:T(8,128)(2,1)S(1)} %copy.44, bf16[8,80,16]{2,1,0:T(8,128)(2,1)S(1)} %copy.45, bf16[8,80,32]{2,1,0:T(8,128)(2,1)S(1)} %copy.46, bf16[8,80,16]{2,1,0:T(8,128)(2,1)S(1)} %copy.47, bf16[8,80,16]{2,1,0:T(8,128)(2,1)S(1)} %copy.48, ...), dimensions={2} | concatenate | bytes 1310720 | tf_op jit(solution)/shard_map/concatenate | solution.py:425
  24.9 0.0 all-to-all-done.x_ref
  24.9 4.8 %all-to-all-start.1 = ((bf16[8,80,512]{2,1,0:T(8,128)(2,1)}), bf16[8,80,512]{2,1,0:T(8,128)(2,1)S(1)}, u32[]{:S(2)}, u32[]{:S(2)}) async-start(bf16[8,80,512]{2,1,0:T(8,128)(2,1)} %concatenate.11), calls=%async_computation.1 | async-start | bytes 1310720 | tf_op jit(solution)/shard_map/all_to_all | solution.py:441
  29.8 0.1 pad.12.clone
  29.8 0.2 convolution_convert_fusion
  30.0 0.7 maximum_maximum_fusion.we_ref
  30.8 3.4 %weights.1 = (bf16[544,256]{1,0:T(8,128)(2,1)}, bf16[512,512]{1,0:T(8,128)(2,1)}) custom-call(bf16[128,512]{1,0:T(8,128)(2,1)} %maximum_maximum_fusion.we_ref, bf16[3,512]{1,0:T(4,128)(2,1)} %queries_ref.3, bf16[512,1024]{1,0:T(8,128)(2,1)} %wkv_ref.3, bf16[512,512]{1,0:T(8,128)(2,1)} %wout_ref.1), custom_call_target="tpu_custom_call" | custom-call | tf_op jit(solution)/shard_map/weights/pallas_call | solution.py:446
  34.2 0.6 add_convert_fusion.edge_ref
  34.8 15.9 %pool.1 = (bf16[32,3,16,512]{3,2,1,0:T(8,128)(2,1)}, bf16[2816,128]{1,0:T(8,128)(2,1)}) custom-call(bf16[8,80,512]{2,1,0:T(8,128)(2,1)} %copy-done.2, bf16[32,3,16,512]{3,2,1,0:T(8,128)(2,1)} %bitcast.81, bf16[544,256]{1,0:T(8,128)(2,1)} %get-tuple-element.14.w2_ref, bf16[512,512]{1,0:T(8,128)(2,1)} %get-tuple-element.15.woutp_ref), custom_call_target="tpu_custom_call" | custom-call | tf_op jit(solution)/shard_map/pool/pallas_call | solution.py:459
  50.7 0.0 copy-start.1
  50.7 0.8 copy-done.1
  51.5 45.3 %windows.1 = (bf16[4,384,512]{2,1,0:T(8,128)(2,1)}, bf16[16,176,128]{2,1,0:T(8,128)(2,1)}) custom-call(bf16[16,176,128]{2,1,0:T(8,128)(2,1)} %bitcast.82, s32[2]{0:T(128)} %add_convert_fusion.edge_ref, bf16[8,80,512]{2,1,0:T(8,128)(2,1)} %copy-done.1, bf16[32,3,16,512]{3,2,1,0:T(8,128)(2,1)} %get-tuple-element.17.latent_ref, ...), custom_call_target="tpu_custom_call" | custom-call | tf_op jit(solution)/shard_map/windows/pallas_call | solution.py:485
  96.8 8.0 %finish.1 = (bf16[32,3,16,512]{3,2,1,0:T(8,128)(2,1)}, f32[80,512]{1,0:T(8,128)}, f32[512,1024]{1,0:T(8,128)}, f32[512,512]{1,0:T(8,128)}) custom-call(bf16[4,384,512]{2,1,0:T(8,128)(2,1)} %get-tuple-element.18.att_ref, bf16[32,3,16,512]{3,2,1,0:T(8,128)(2,1)} %get-tuple-element.17.latent_ref, bf16[512,512]{1,0:T(8,128)(2,1)} %wproj_ref.1, ...), custom_call_target="tpu_custom_call" | custom-call | tf_op jit(solution)/shard_map/finish/pallas_call | solution.py:505
  (29 shorter events, 0.2 us)
Async XLA Ops:
  0.6 29.2 %copy-start = (bf16[13,512]{1,0:T(8,128)(2,1)S(1)}, bf16[13,512]{1,0:T(8,128)(2,1)}, u32[]{:S(2)}) copy-start(bf16[13,512]{1,0:T(8,128)(2,1)} %param.13) | copy-start | bytes 39940
  2.4 9.9 %collective-permute-start = (bf16[80,4,128]{0,2,1:T(8,128)(2,1)S(1)}, bf16[80,4,128]{0,2,1:T(8,128)(2,1)S(1)}, u32[]{:S(2)}, u32[]{:S(2)}) collective-permute-start(bf16[80,4,128]{0,2,1:T(8,128)(2,1)S(1)} %get-tuple-element.27), channel_id=1, source_target_pairs={{0,1},{1,2},{2,3},{3,4},{4,5},{5,6},{6,7},{7,8},{8,9},{9,10},{10,1... | collective-permute-start | bytes 245768 | tf_op jit(solution)/shard_map/ppermute | solution.py:436
  6.8 5.9 %collective-permute-start.1 = (bf16[80,4,128]{0,2,1:T(8,128)(2,1)S(1)}, bf16[80,4,128]{0,2,1:T(8,128)(2,1)S(1)}, u32[]{:S(2)}, u32[]{:S(2)}) collective-permute-start(bf16[80,4,128]{0,2,1:T(8,128)(2,1)S(1)} %get-tuple-element.28), channel_id=1, source_target_pairs={{1,0},{2,1},{3,2},{4,3},{5,4},{6,5},{7,6},{8,7},{9,8},{10,9},{11,1... | collective-permute-start | bytes 245768 | tf_op jit(solution)/shard_map/ppermute | solution.py:437
  8.2 16.8 %all-to-all-start = ((bf16[8,80,512]{2,1,0:T(8,128)(2,1)}), bf16[8,80,512]{2,1,0:T(8,128)(2,1)S(1)}, u32[]{:S(2)}, u32[]{:S(2)}) async-start(bf16[8,80,512]{2,1,0:T(8,128)(2,1)} %copy.21), calls=%async_computation | async-start | bytes 1310720 | tf_op jit(solution)/shard_map/all_to_all | solution.py:439
  21.2 8.6 %copy-start.4 = (s32[8]{0:T(128)S(1)}, s32[8]{0:T(128)}, u32[]{:S(2)}) copy-start(s32[8]{0:T(128)} %param.12) | copy-start | bytes 100
  21.2 8.8 %copy-start.3 = (bf16[80,512]{1,0:T(8,128)(2,1)S(1)}, bf16[80,512]{1,0:T(8,128)(2,1)}, u32[]{:S(2)}) copy-start(bf16[80,512]{1,0:T(8,128)(2,1)} %param.14) | copy-start | bytes 245764
  24.9 9.3 %copy-start.2 = (bf16[8,80,512]{2,1,0:T(8,128)(2,1)}, bf16[8,80,512]{2,1,0:T(8,128)(2,1)S(1)}, u32[]{:S(2)}) copy-start(bf16[8,80,512]{2,1,0:T(8,128)(2,1)S(1)} %all-to-all-done.x_ref) | copy-start | bytes 1966084
  24.9 25.8 %all-to-all-start.1 = ((bf16[8,80,512]{2,1,0:T(8,128)(2,1)}), bf16[8,80,512]{2,1,0:T(8,128)(2,1)S(1)}, u32[]{:S(2)}, u32[]{:S(2)}) async-start(bf16[8,80,512]{2,1,0:T(8,128)(2,1)} %concatenate.11), calls=%async_computation.1 | async-start | bytes 1310720 | tf_op jit(solution)/shard_map/all_to_all | solution.py:441
  50.7 0.8 copy-start.1

commit v2 on v1

--- a/solution.py
+++ b/solution.py
@@ -34,6 +34,14 @@
     return high, (value - high.astype(F32)).astype(BF)
 
 
+def place(lev, tile):
+    return {"lev": lev, "tile": tile}
+
+
+def remote(src, dst, send, recv, device):
+    return pltpu.make_async_remote_copy(src_ref=src, dst_ref=dst, send_sem=send, recv_sem=recv, device_id=device, device_id_type=pl.DeviceIdType.MESH)
+
+
 def query_rows(queries):
     rows = jnp.concatenate([jnp.broadcast_to(queries[q : q + 1], (HEADS, D)) for q in range(LATENT)], axis=0)
     head = lax.broadcasted_iota(jnp.int32, (LATENT * HEADS, D), 0) % HEADS
@@ -41,7 +49,7 @@
     return jnp.where(head == lane, rows, 0.0)
 
 
-def weights_kernel(we_ref, queries_ref, wkv_ref, wout_ref, w2_ref, woutp_ref):
+def fold_weights(we_ref, queries_ref, wkv_ref, wout_ref, w2_ref, woutp_ref):
     row = lax.broadcasted_iota(jnp.int32, (D, D), 0)
     lane = lax.broadcasted_iota(jnp.int32, (D, D), 1)
     mix = jnp.where(lane == (row % HEADS) * HD + row // HEADS, 1.0, 0.0).astype(BF)
@@ -85,10 +93,137 @@
     return pairs, [(e * inverse).astype(BF).astype(F32) for e in expo]
 
 
-def pool_kernel(x_ref, d_ref, w2_ref, woutp_ref, latent_ref, terms_ref, vals_ref, dpool_ref, pooled_ref, dv_ref, tacc_ref, gacc_ref):
-    step = pl.program_id(0)
-    pairs, probs = forward_levels(lambda l: x_ref[l], w2_ref, vals_ref)
-    d_rows = jnp.concatenate([d_ref[:, q].reshape(128, D) for q in range(LATENT)], axis=0)
+def select(rows, lanes, want):
+    row = lax.broadcasted_iota(jnp.int32, (rows, lanes), 0)
+    return jnp.where(row == want, 1.0, 0.0).astype(BF)
+
+
+def lane_ids(lanes, start=0):
+    return lax.broadcasted_iota(jnp.int32, (1, lanes), 1) + start
+
+
+def inside_row(lon, lat):
+    return jnp.where((lat >= 0) & (lat < 128), lon * 128 + lat, -1)
+
+
+def exchange_stages(x_ref, pixels_ref, xa_ref, xb_ref, own_ref, near_ref, side_ref, mine_ref, rim_ref, send_sem, recv_sem):
+    lev, tile = lax.axis_index("lev"), lax.axis_index("tile")
+    bands, tiles = lax.axis_size("lev"), lax.axis_size("tile")
+    next_tile, last_tile = lax.rem(tile + 1, tiles), lax.rem(tile + tiles - 1, tiles)
+    levs = [lax.rem(lev + off, bands) for off in range(bands)]
+
+    def copy(src, dst, slot, device):
+        return remote(src, dst, send_sem.at[slot], recv_sem.at[slot], device)
+
+    own, near, east, west = [], [], [], []
+    for off in range(1, bands):
+        own.append(copy(own_ref.at[levs[off]], mine_ref.at[lev], off - 1, place(levs[off], tile)))
+        near.append(copy(near_ref.at[levs[off]], rim_ref.at[lev, :, 256:512], off + 6, place(levs[off], tile)))
+    for off in range(bands):
+        east.append(copy(side_ref.at[0, levs[off]], rim_ref.at[lev, :, 0:128], 14 + off, place(levs[off], next_tile)))
+        west.append(copy(side_ref.at[1, levs[off]], rim_ref.at[lev, :, 128:256], 22 + off, place(levs[off], last_tile)))
+
+    def greet():
+        barrier = pltpu.get_barrier_semaphore()
+        for off in range(1, bands):
+            pl.semaphore_signal(barrier, inc=1, device_id=place(levs[off], tile), device_id_type=pl.DeviceIdType.MESH)
+        for off in range(bands):
+            for side in (next_tile, last_tile):
+                pl.semaphore_signal(barrier, inc=1, device_id=place(levs[off], side), device_id_type=pl.DeviceIdType.MESH)
+
+    def send_own():
+        pixels_ref[...] = x_ref[...].reshape(F * 32, 128).astype(F32)
+        for lon in range(32):
+            plane = pixels_ref[pl.ds(lon, F, stride=32), :].astype(BF)
+            xa_ref[(lon // 8) * F : (lon // 8 + 1) * F, (lon % 8) * 128 : (lon % 8 + 1) * 128] = plane
+            moved = (lon + 4) % 32
+            xb_ref[(moved // 8) * F : (moved // 8 + 1) * F, (moved % 8) * 128 : (moved % 8 + 1) * 128] = plane
+        rows = xa_ref[...]
+        for two in range(bands // 2):
+            j = lane_ids(256)
+            want = ((j % 128) // 16) * 128 + 16 * (2 * two + j // 128) + j % 16
+            out = dot(rows, select(1024, 256, want)).astype(BF)
+            for c in range(4):
+                for half in range(2):
+                    own_ref[2 * two + half, :, c * 128 : (c + 1) * 128] = out[c * F : (c + 1) * F, half * 128 : (half + 1) * 128]
+        pl.semaphore_wait(pltpu.get_barrier_semaphore(), 3 * bands - 1)
+        for c in own:
+            c.start()
+        mine_ref[lev] = own_ref[lev]
+
+    def send_rim():
+        rows = xb_ref[...]
+        for four in range(2):
+            j = lane_ids(256)
+            band = 4 * four + j // 64
+            lat = 16 * band + j % 4 + jnp.where(j % 64 < 32, -4, 16)
+            out = dot(rows, select(1024, 256, inside_row((j % 32) // 4, lat))).astype(BF)
+            for b in range(4):
+                lanes = slice(64 * b, 64 * b + 64)
+                for c in range(2):
+                    pair = [out[k * F : (k + 1) * F, lanes] for k in (2 * c, 2 * c + 1)]
+                    near_ref[4 * four + b, :, c * 128 : (c + 1) * 128] = jnp.concatenate(pair, axis=1)
+        for c in near:
+            c.start()
+        rows = jnp.concatenate([xb_ref[0:F, 0:512], xb_ref[0:F, 512:1024]], axis=0)
+        for two in range(bands // 2):
+            j = lane_ids(256)
+            k = j % 128
+            thin = k % 16
+            wide = k - 32
+            lat = jnp.where(k < 16, 4 + thin % 4, jnp.where(k < 32, thin % 4, jnp.where(k < 64, 8 + wide % 8, jnp.where(k < 80, 16 + thin % 4, 20 + thin % 4))))
+            lon = jnp.where((k >= 32) & (k < 64), wide // 8, thin // 4)
+            lat = jnp.where(k < 96, 16 * (2 * two + j // 128) - 4 + lat, -1)
+            out = dot(rows, select(512, 256, inside_row(lon, lat))).astype(BF)
+            for side in range(2):
+                for half in range(2):
+                    side_ref[side, 2 * two + half] = out[side * F : (side + 1) * F, half * 128 : (half + 1) * 128]
+        for c in east + west:
+            c.start()
+        rim_ref[lev, :, 256:512] = near_ref[lev]
+
+    def take_own():
+        for c in own:
+            c.wait_recv()
+
+    def take_rim():
+        for c in near + east + west:
+            c.wait_recv()
+        for c in own + near + east + west:
+            c.wait_send()
+
+    return greet, send_own, send_rim, take_own, take_rim
+
+
+def pool_kernel(x_ref, d_ref, we_ref, queries_ref, wkv_ref, wout_ref, latent_ref, terms_ref, w2_ref, woutp_ref, far_ref, vals_ref, dpool_ref, pooled_ref, dv_ref, tacc_ref, gacc_ref, pixels_ref, xa_ref, xb_ref, own_ref, near_ref, side_ref, mine_ref, rim_ref, send_sem, recv_sem):
+    greet, send_own, send_rim, take_own, take_rim = exchange_stages(x_ref, pixels_ref, xa_ref, xb_ref, own_ref, near_ref, side_ref, mine_ref, rim_ref, send_sem, recv_sem)
+    greet()
+    send_own()
+    send_rim()
+    fold_weights(we_ref, queries_ref, wkv_ref, wout_ref, w2_ref, woutp_ref)
+    tacc_ref[...] = jnp.zeros_like(tacc_ref)
+    gacc_ref[...] = jnp.zeros_like(gacc_ref)
+    take_own()
+
+    def group_loop(group, carry):
+        pool_group(group, mine_ref, d_ref, w2_ref, woutp_ref, latent_ref, vals_ref, dpool_ref, pooled_ref, dv_ref, tacc_ref, gacc_ref)
+        return carry
+
+    lax.fori_loop(0, 4, group_loop, 0)
+    for h in range(HEADS):
+        for j in range(4):
+            terms_ref[j * D + h * HD : j * D + (h + 1) * HD, :] = gacc_ref[pl.ds(j * D + h, HD, stride=HEADS), :].astype(BF)
+        terms_ref[4 * D + h * HD : 4 * D + (h + 1) * HD, :] = tacc_ref[pl.ds(h, HD, stride=HEADS), :].astype(BF)
+    terms_ref[5 * D : 5 * D + MV - D, :] = tacc_ref[D:MV, :].astype(BF)
+    terms_ref[5 * D + MV - D :, :] = jnp.zeros((TERMS - 5 * D - MV + D, KX), BF)
+    take_rim()
+    far_ref[...] = rim_ref[...]
+
+
+def pool_group(group, x_ref, d_ref, w2_ref, woutp_ref, latent_ref, vals_ref, dpool_ref, pooled_ref, dv_ref, tacc_ref, gacc_ref):
+    lane0 = pl.multiple_of(group * 128, 128)
+    pairs, probs = forward_levels(lambda l: x_ref[l, :, pl.ds(lane0, 128)], w2_ref, vals_ref)
+    d_rows = jnp.concatenate([d_ref[pl.ds(8 * group, 8), q].reshape(128, D) for q in range(LATENT)], axis=0)
     dpool_ref[...] = dot(woutp_ref[...], d_rows, 1, 1)
     parts = [[probs[l][q * HEADS : (q + 1) * HEADS] for q in range(LATENT)] for l in range(LEVELS)]
 
@@ -142,11 +277,6 @@
         lanes = slice((l % 2) * 128, (l % 2) * 128 + 128)
         dv_ref[l // 2, D:MV, lanes] = jnp.concatenate(ds + [zero], axis=0).astype(BF)
 
-    @pl.when(step == 0)
-    def _():
-        tacc_ref[...] = jnp.zeros_like(tacc_ref)
-        gacc_ref[...] = jnp.zeros_like(gacc_ref)
-
     terms = dot(dv_ref[0], pairs[0], 1, 1)
     for pair in range(1, LEVELS // 2):
         terms = terms + dot(dv_ref[pair], pairs[pair], 1, 1)
@@ -157,16 +287,7 @@
         gacc_ref[j * D : (j + 1) * D, :] += gterm[:, j * 128 : (j + 1) * 128]
     latent = dot(pooled, woutp_ref[...], 0, 0).astype(BF)
     for q in range(LATENT):
-        latent_ref[:, q] = latent[q * 128 : (q + 1) * 128].reshape(8, 16, D)
-
-    @pl.when(step == pl.num_programs(0) - 1)
-    def _():
-        for h in range(HEADS):
-            for j in range(4):
-                terms_ref[j * D + h * HD : j * D + (h + 1) * HD, :] = gacc_ref[pl.ds(j * D + h, HD, stride=HEADS), :].astype(BF)
-            terms_ref[4 * D + h * HD : 4 * D + (h + 1) * HD, :] = tacc_ref[pl.ds(h, HD, stride=HEADS), :].astype(BF)
-        terms_ref[5 * D : 5 * D + MV - D, :] = tacc_ref[D:MV, :].astype(BF)
-        terms_ref[5 * D + MV - D :, :] = jnp.zeros((TERMS - 5 * D - MV + D, KX), BF)
+        latent_ref[pl.ds(8 * group, 8), q] = latent[q * 128 : (q + 1) * 128].reshape(8, 16, D)
 
 
 def normalise(values, gain):
@@ -193,16 +314,12 @@
     return jnp.where(src == want, 1.0, 0.0).astype(BF)
 
 
-def place(lev, tile):
-    return {"lev": lev, "tile": tile}
-
-
 def sum_stages(terms_ref, part_ref, band_ref, full_ref, send_sem, recv_sem):
     lev, tile = lax.axis_index("lev"), lax.axis_index("tile")
     bands, tiles = lax.axis_size("lev"), lax.axis_size("tile")
 
     def copy(src, dst, slot, device):
-        return pltpu.make_async_remote_copy(src_ref=src, dst_ref=dst, send_sem=send_sem.at[slot], recv_sem=recv_sem.at[slot], device_id=device, device_id_type=pl.DeviceIdType.MESH)
+        return remote(src, dst, send_sem.at[slot], recv_sem.at[slot], device)
 
     tile_peers = [place(lev, lax.rem(tile + off, tiles)) for off in range(1, tiles)]
     lev_peers = [place(lax.rem(lev + off, bands), tile) for off in range(1, bands)]
@@ -283,18 +400,36 @@
         def _():
             first = group * 3
             for q in range(LATENT):
-                kv_ref[first, 48 + 48 * q : 96 + 48 * q, :] = kv[q * 128 : q * 128 + 48]
-                kv_ref[first + 1, 96 + 32 * q : 128 + 32 * q, :] = kv[q * 128 + 48 : q * 128 + 80]
-                kv_ref[first + 2, 48 + 48 * q : 96 + 48 * q, :] = kv[q * 128 + 80 : q * 128 + 128]
-
-        @pl.when(group >= 2)
+                row = q * 128
+                kv_ref[first, 48 + 32 * q : 80 + 32 * q, :] = kv[row : row + 32]
+                kv_ref[first + 1, 96 + 32 * q : 128 + 32 * q, :] = kv[row + 32 : row + 64]
+                kv_ref[first + 2, 48 + 32 * q : 80 + 32 * q, :] = kv[row + 64 : row + 96]
+
+        @pl.when(group == 2)
         def _():
-            first = 6 + (group - 2) * 6
-            for half in range(2):
-                for q in range(LATENT):
-                    row = q * 128 + half * 64
-                    kv_ref[first + 3 * half, 96 + 32 * q : 128 + 32 * q, :] = kv[row : row + 32]
-                    kv_ref[first + 3 * half + 2, 96 + 32 * q : 128 + 32 * q, :] = kv[row + 32 : row + 64]
+            for q in range(LATENT):
+                row = q * 128
+                near = slice(144 + 16 * q, 160 + 16 * q)
+                kv_ref[3, near, :] = kv[row : row + 16]
+                kv_ref[0, near, :] = kv[row + 16 : row + 32]
+                kv_ref[5, near, :] = kv[row + 32 : row + 48]
+                kv_ref[2, near, :] = kv[row + 48 : row + 64]
+
+        def column_rim(half, column):
+            for q in range(LATENT):
+                row = q * 128 + half * 64
+                near = slice(96 + 32 * q, 128 + 32 * q)
+                kv_ref[3 + 3 * column, near, :] = kv[row : row + 32]
+                kv_ref[5 + 3 * column, near, :] = kv[row + 32 : row + 64]
+
+        @pl.when(group == 2)
+        def _():
+            column_rim(1, 1)
+
+        @pl.when(group == 3)
+        def _():
+            column_rim(0, 2)
+            column_rim(1, 3)
         return carry
 
     lax.fori_loop(0, 4, halo, 0)
@@ -343,7 +478,7 @@
 
     inside = (edge_ref[0] == 0, edge_ref[1] == 0)
     plain = [(key < 96) | ok for ok in inside]
-    corner = [(key < 48) | (key % 48 < 16) | ok for ok in inside]
+    corner = [(key < 48) | ((key < 144) & ((key + 16) % 32 < 16)) | ok for ok in inside]
 
     for side in range(2):
         first = 3 * (1 - side)
@@ -407,66 +542,21 @@
     return pltpu.CompilerParams(vmem_limit_bytes=VMEM_LIMIT, **kw)
 
 
-def halo_positions(ext):
-    bands = ext.reshape(F, 40, 17, 8)
-    low, mid, high = (bands[:, :, wa : wa + 15 : 2] for wa in range(3))
-
-    def flat(block):
-        return block.transpose(2, 0, 1, 3).reshape(LEVELS, F, -1)
-
-    pieces = []
-    for far, near in ((slice(0, 4), slice(4, 8)), (slice(36, 40), slice(32, 36))):
-        pieces += [flat(low[:, far, :, 4:]), flat(low[:, far, :, :4]), flat(low[:, near, :, :4])]
-        pieces += [flat(mid[:, far])]
-        pieces += [flat(high[:, far, :, :4]), flat(high[:, far, :, 4:]), flat(high[:, near, :, 4:])]
-    for c in (1, 2, 3):
-        pieces += [flat(low[:, 8 * c : 8 * c + 8, :, :4]), flat(high[:, 8 * c : 8 * c + 8, :, 4:])]
-    pieces.append(jnp.zeros((LEVELS, F, 64), ext.dtype))
-    return jnp.concatenate(pieces, axis=2)
-
-
 def per_device(inputs, level_ids, level_table, w_embed, queries, w_kv, w_out, gain, w_qkv, w_proj, d_latent):
     band = lax.axis_index("lev")
     bands = lax.axis_size("lev")
     tiles = lax.axis_size("tile")
     lon_rows, lat_rows = d_latent.shape[:2]
-    x = inputs[0]
-    ring = [(i, (i + 1) % tiles) for i in range(tiles)]
-    back = [(target, source) for source, target in ring]
-    west = lax.ppermute(x[:, 28:32], "tile", ring)
-    east = lax.ppermute(x[:, 0:4], "tile", back)
-    own = x.reshape(F, 32, 8, 16).transpose(2, 0, 1, 3).reshape(LEVELS, F, 512)
-    own = lax.all_to_all(own, "lev", split_axis=0, concat_axis=0, tiled=True)
-    ext = jnp.pad(jnp.concatenate([west, x, east], axis=1), ((0, 0), (0, 0), (4, 4)))
-    far = lax.all_to_all(halo_positions(ext), "lev", split_axis=0, concat_axis=0, tiled=True)
-
     onehot = (level_ids[:, None] == jnp.arange(level_table.shape[0], dtype=jnp.int32)[None, :]).astype(BF)
     rows = jnp.dot(onehot, level_table, preferred_element_type=F32).astype(BF)
     we = jnp.concatenate([w_embed, rows, jnp.zeros((KX - F - LEVELS, D), BF)], axis=0)
-    w2, woutp = pl.pallas_call(
-        weights_kernel,
-        out_shape=(whole((MV, 2 * KX), BF), whole((D, D), BF)),
-        compiler_params=params(),
-        name="weights",
-    )(we, queries, w_kv, w_out)
-
+    vmem = pl.BlockSpec(memory_space=pltpu.VMEM)
     d_nat = d_latent.transpose(0, 2, 1, 3)
-    block = pl.BlockSpec((8, LATENT, 16, D), lambda g: (g, 0, 0, 0))
-
-    def fixed(shape):
-        return pl.BlockSpec(shape, lambda g: (0,) * len(shape))
-
-    latent, terms = pl.pallas_call(
+    latent, terms, w2, woutp, far = pl.pallas_call(
         pool_kernel,
-        grid=(4,),
-        in_specs=[
-            pl.BlockSpec((LEVELS, F, 128), lambda g: (0, 0, g)),
-            block,
-            fixed((MV, 2 * KX)),
-            fixed((D, D)),
-        ],
-        out_specs=[block, fixed((TERMS, KX))],
-        out_shape=(whole(d_nat.shape, BF), whole((TERMS, KX), BF)),
+        in_specs=[vmem] * 6,
+        out_specs=(vmem,) * 5,
+        out_shape=(whole(d_nat.shape, BF), whole((TERMS, KX), BF), whole((MV, 2 * KX), BF), whole((D, D), BF), whole((LEVELS, F, 512), BF)),
         scratch_shapes=[
             pltpu.VMEM((LEVELS, D, 128), F32),
             pltpu.VMEM((D, 384), F32),
@@ -474,14 +564,23 @@
             pltpu.VMEM((LEVELS // 2, MV, 256), BF),
             pltpu.VMEM((MV, KX), F32),
             pltpu.VMEM((4 * D, 128), F32),
+            pltpu.VMEM((F * 32, 128), F32),
+            pltpu.VMEM((4 * F, 1024), BF),
+            pltpu.VMEM((4 * F, 1024), BF),
+            pltpu.VMEM((LEVELS, F, 512), BF),
+            pltpu.VMEM((LEVELS, F, 256), BF),
+            pltpu.VMEM((2, LEVELS, F, 128), BF),
+            pltpu.VMEM((LEVELS, F, 512), BF),
+            pltpu.VMEM((LEVELS, F, 512), BF),
+            pltpu.SemaphoreType.DMA((30,)),
+            pltpu.SemaphoreType.DMA((30,)),
         ],
-        compiler_params=params(dimension_semantics=("arbitrary",)),
+        compiler_params=params(collective_id=2, has_side_effects=True),
         name="pool",
-    )(own, d_nat, w2, woutp)
+    )(inputs[0], d_nat, we, queries, w_kv, w_out)
 
     factor = 1.0 / math.sqrt(lon_rows * lat_rows * bands * tiles)
     edge = jnp.stack([band == 0, band == bands - 1]).astype(jnp.int32)
-    vmem = pl.BlockSpec(memory_space=pltpu.VMEM)
     att, total = pl.pallas_call(
         window_kernel,
         in_specs=[vmem, pl.BlockSpec(memory_space=pltpu.SMEM)] + [vmem] * 6,

time: 105 us -> 87.9 us (0.84)
  local copies, waits for them, and re-layouts: 15.6 us -> 0.12 us
  starting transfers between devices: 13.3 us -> 0 us
  Pallas kernels: 72.6 us -> 83.8 us
    pallas_call x2 -> x1, Pallas kernels: 19.3 us -> 30.3 us  [per_device(): pl.pallas_call(pool_kernel, in_specs=[vmem] * 6, out_specs=(vmem,) * 5, o...]
    all_to_all x2 -> x0, starting transfers between devices: 8.96 us -> none  [the longest x1 4.82 us: per_device(): lax.all_to_all(halo_positions(ext), 'lev', split_axis=0, concat_axis=0, t...]
    reshape x22 -> x0, local copies, waits for them, and re-layouts: 6.86 us -> none  [the longest x21 5.64 us: flat(): return block.transpose(2, 0, 1, 3).reshape(LEVELS, F, -1)]
    ppermute x2 -> x0, starting transfers between devices: 4.38 us -> none  [the longest x1 4.37 us: per_device(): west = lax.ppermute(x[:, 28:32], 'tile', ring)]
    concatenate x1 -> x0, local copies, waits for them, and re-layouts: 3.69 us -> none  [halo_positions(): return jnp.concatenate(pieces, axis=2)]
    unnamed x11 -> x2, local copies, waits for them, and re-layouts: 2.55 us -> 0.04 us
    transpose x22 -> x0, local copies, waits for them, and re-layouts: 1.31 us -> none  [the longest x21 1.12 us: flat(): return block.transpose(2, 0, 1, 3).reshape(LEVELS, F, -1)]
  transfers between devices with their start and end apart: 4 -> 0, of which waited for: 1 -> 0; matrix products, arithmetic and copies ran while one was open for 14% -> 0% of each run, Pallas kernels for 18% -> 0%
where the time goes in v2:
time: 87.9 us; the launch traced here: 87.7 us
  Pallas kernels  83.8 us (95%)
  other arithmetic  2.23 us (3%)
    pallas_call x1, Pallas kernels, per_device(): pl.pallas_call(window_kernel, in_specs=[vmem, pl.BlockSpec(memory_space=p...  45.5 us
    pallas_call x1, Pallas kernels, per_device(): pl.pallas_call(pool_kernel, in_specs=[vmem] * 6, out_specs=(vmem,) * 5, o...  30.3 us
    pallas_call x1, Pallas kernels, per_device(): pl.pallas_call(functools.partial(finish_kernel, factor=factor), out_shape...  8.02 us

profile of v2, /device:TPU:1, one launch (start us, length us, event | category | flops | bytes accessed | tf_op | source)
XLA Modules:
  0.0 87.7 jit_solution(13132767340843802750)
XLA Ops:
  0.6 0.0 copy-start
  0.7 0.6 add_convert_fusion.edge_ref
  1.2 0.1 pad.4.clone
  1.3 0.0 copy-done
  1.4 0.8 convolution_convert_fusion
  2.2 1.6 %maximum_maximum_fusion.we_ref = bf16[128,512]{1,0:T(8,128)(2,1)} fusion(bf16[8,512]{1,0:T(8,128)(2,1)S(1)} %convolution_convert_fusion, bf16[80,512]{1,0:T(8,128)(2,1)} %param.14, bf16[128]{0:T(256)(128)(2,1)S(1)} %pad.4.clone), kind=kLoop, calls=%fused_computation.1 | loop fusion | flops 393216 | bytes 221440 | tf_op jit(solution)/shard_map/concatenate | solution.py:552
  3.8 30.3 %pool.1 = (bf16[32,3,16,512]{3,2,1,0:T(8,128)(2,1)}, bf16[2816,128]{1,0:T(8,128)(2,1)}, bf16[544,256]{1,0:T(8,128)(2,1)}, bf16[512,512]{1,0:T(8,128)(2,1)}, bf16[8,80,512]{2,1,0:T(8,128)(2,1)}) custom-call(bf16[80,32,128]{2,1,0:T(8,128)(2,1)} %bitcast.12, bf16[32,3,16,512]{3,2,1,0:T(8,128)(2,1)} %bitcast.9, bf16[128,512]{1,0:T(8,128)(2,1)} %maximum_maximum_fusion.we_ref, ...), custom_call_target="tpu_custom_call" | custom-call | tf_op jit(solution)/shard_map/pool/pallas_call | solution.py:555
  34.1 45.5 %windows.1 = (bf16[4,384,512]{2,1,0:T(8,128)(2,1)}, bf16[16,176,128]{2,1,0:T(8,128)(2,1)}) custom-call(bf16[16,176,128]{2,1,0:T(8,128)(2,1)} %bitcast.11, s32[2]{0:T(128)} %add_convert_fusion.edge_ref, bf16[8,80,512]{2,1,0:T(8,128)(2,1)} %get-tuple-element.16.xh_ref, bf16[32,3,16,512]{3,2,1,0:T(8,128)(2,1)} %get-tuple-element.17.latent_ref, ...), custom_call_target="tpu_custom_call" | custom-call | tf_op jit(solution)/shard_map/windows/pallas_call | solution.py:584
  79.7 8.0 %finish.1 = (bf16[32,3,16,512]{3,2,1,0:T(8,128)(2,1)}, f32[80,512]{1,0:T(8,128)}, f32[512,1024]{1,0:T(8,128)}, f32[512,512]{1,0:T(8,128)}) custom-call(bf16[4,384,512]{2,1,0:T(8,128)(2,1)} %get-tuple-element.20.att_ref, bf16[32,3,16,512]{3,2,1,0:T(8,128)(2,1)} %get-tuple-element.17.latent_ref, bf16[512,512]{1,0:T(8,128)(2,1)} %wproj_ref.1, ...), custom_call_target="tpu_custom_call" | custom-call | tf_op jit(solution)/shard_map/finish/pallas_call | solution.py:604
  (1 shorter events, 0.0 us)
Async XLA Ops:
  0.6 0.7 copy-start

commit v3 on v2

--- a/solution.py
+++ b/solution.py
@@ -49,7 +49,15 @@
     return jnp.where(head == lane, rows, 0.0)
 
 
-def fold_weights(we_ref, queries_ref, wkv_ref, wout_ref, w2_ref, woutp_ref):
+def fold_weights(ids_ref, table_ref, embed_ref, queries_ref, wkv_ref, wout_ref, w2_ref, woutp_ref, we_ref):
+    slab = lax.broadcasted_iota(jnp.int32, (16, 1), 0)
+    wanted = jnp.full((16, 1), -1, jnp.int32)
+    for l in range(LEVELS):
+        wanted = jnp.where(slab == l, ids_ref[l], wanted)
+    onehot = jnp.where(lax.broadcasted_iota(jnp.int32, (16, 16), 1) == wanted, 1.0, 0.0).astype(BF)
+    we_ref[0:F, :] = embed_ref[...]
+    we_ref[F : F + 16, :] = dot(onehot, table_ref[...]).astype(BF)
+    we_ref[F + 16 :, :] = jnp.zeros((KX - F - 16, D), BF)
     row = lax.broadcasted_iota(jnp.int32, (D, D), 0)
     lane = lax.broadcasted_iota(jnp.int32, (D, D), 1)
     mix = jnp.where(lane == (row % HEADS) * HD + row // HEADS, 1.0, 0.0).astype(BF)
@@ -151,7 +159,7 @@
             c.start()
         mine_ref[lev] = own_ref[lev]
 
-    def send_rim():
+    def sort_rim():
         rows = xb_ref[...]
         for four in range(2):
             j = lane_ids(256)
@@ -163,8 +171,6 @@
                 for c in range(2):
                     pair = [out[k * F : (k + 1) * F, lanes] for k in (2 * c, 2 * c + 1)]
                     near_ref[4 * four + b, :, c * 128 : (c + 1) * 128] = jnp.concatenate(pair, axis=1)
-        for c in near:
-            c.start()
         rows = jnp.concatenate([xb_ref[0:F, 0:512], xb_ref[0:F, 512:1024]], axis=0)
         for two in range(bands // 2):
             j = lane_ids(256)
@@ -178,13 +184,13 @@
             for side in range(2):
                 for half in range(2):
                     side_ref[side, 2 * two + half] = out[side * F : (side + 1) * F, half * 128 : (half + 1) * 128]
-        for c in east + west:
-            c.start()
         rim_ref[lev, :, 256:512] = near_ref[lev]
 
     def take_own():
         for c in own:
             c.wait_recv()
+        for c in near + east + west:
+            c.start()
 
     def take_rim():
         for c in near + east + west:
@@ -192,15 +198,15 @@
         for c in own + near + east + west:
             c.wait_send()
 
-    return greet, send_own, send_rim, take_own, take_rim
-
-
-def pool_kernel(x_ref, d_ref, we_ref, queries_ref, wkv_ref, wout_ref, latent_ref, terms_ref, w2_ref, woutp_ref, far_ref, vals_ref, dpool_ref, pooled_ref, dv_ref, tacc_ref, gacc_ref, pixels_ref, xa_ref, xb_ref, own_ref, near_ref, side_ref, mine_ref, rim_ref, send_sem, recv_sem):
-    greet, send_own, send_rim, take_own, take_rim = exchange_stages(x_ref, pixels_ref, xa_ref, xb_ref, own_ref, near_ref, side_ref, mine_ref, rim_ref, send_sem, recv_sem)
+    return greet, send_own, sort_rim, take_own, take_rim
+
+
+def pool_kernel(ids_ref, x_ref, d_ref, table_ref, embed_ref, queries_ref, wkv_ref, wout_ref, latent_ref, terms_ref, w2_ref, woutp_ref, far_ref, we_ref, vals_ref, dpool_ref, pooled_ref, dv_ref, tacc_ref, gacc_ref, pixels_ref, xa_ref, xb_ref, own_ref, near_ref, side_ref, mine_ref, rim_ref, send_sem, recv_sem):
+    greet, send_own, sort_rim, take_own, take_rim = exchange_stages(x_ref, pixels_ref, xa_ref, xb_ref, own_ref, near_ref, side_ref, mine_ref, rim_ref, send_sem, recv_sem)
     greet()
     send_own()
-    send_rim()
-    fold_weights(we_ref, queries_ref, wkv_ref, wout_ref, w2_ref, woutp_ref)
+    sort_rim()
+    fold_weights(ids_ref, table_ref, embed_ref, queries_ref, wkv_ref, wout_ref, w2_ref, woutp_ref, we_ref)
     tacc_ref[...] = jnp.zeros_like(tacc_ref)
     gacc_ref[...] = jnp.zeros_like(gacc_ref)
     take_own()
@@ -314,29 +320,40 @@
     return jnp.where(src == want, 1.0, 0.0).astype(BF)
 
 
-def sum_stages(terms_ref, part_ref, band_ref, full_ref, send_sem, recv_sem):
+def sum_stages(terms_ref, halves_ref, pair_ref, part_ref, band_ref, full_ref, send_sem, recv_sem):
     lev, tile = lax.axis_index("lev"), lax.axis_index("tile")
     bands, tiles = lax.axis_size("lev"), lax.axis_size("tile")
+    groups = tiles // 2
+    group, core = tile // 2, lax.rem(tile, 2)
 
     def copy(src, dst, slot, device):
         return remote(src, dst, send_sem.at[slot], recv_sem.at[slot], device)
 
-    tile_peers = [place(lev, lax.rem(tile + off, tiles)) for off in range(1, tiles)]
+    other = place(lev, 2 * group + 1 - core)
     lev_peers = [place(lax.rem(lev + off, bands), tile) for off in range(1, bands)]
-    first = [copy(terms_ref.at[peer["tile"]], part_ref.at[i], i, peer) for i, peer in enumerate(tile_peers)]
-    second = [copy(band_ref.at[lev], band_ref.at[lev], 15 + i, peer) for i, peer in enumerate(lev_peers)]
-    third = [copy(full_ref.at[tile], full_ref.at[tile], 22 + i, peer) for i, peer in enumerate(tile_peers)]
+    group_ids = [lax.rem(group + off, groups) for off in range(1, groups)]
+    group_peers = [place(lev, 2 * g + core) for g in group_ids]
+    swap = copy(terms_ref.at[1 - core], halves_ref, 0, other)
+    first = [copy(pair_ref.at[g], part_ref.at[i], 1 + i, group_peers[i]) for i, g in enumerate(group_ids)]
+    second = [copy(band_ref.at[lev], band_ref.at[lev], 8 + i, peer) for i, peer in enumerate(lev_peers)]
+    third = [copy(full_ref.at[core, group], full_ref.at[core, group], 15 + i, peer) for i, peer in enumerate(group_peers)]
+    back = copy(full_ref.at[core], full_ref.at[core], 22, other)
 
     def greet():
         barrier = pltpu.get_barrier_semaphore()
-        for peer in tile_peers + lev_peers:
+        for peer in group_peers + lev_peers + [other]:
             pl.semaphore_signal(barrier, inc=1, device_id=peer, device_id_type=pl.DeviceIdType.MESH)
-        pl.semaphore_wait(barrier, tiles + bands - 2)
+        pl.semaphore_wait(barrier, groups + bands - 1)
+        swap.start()
+
+    def over_group():
+        swap.wait_recv()
+        pair_ref[...] = (terms_ref[core].astype(F32) + halves_ref[...].astype(F32)).astype(BF)
         for c in first:
             c.start()
 
     def over_lev():
-        total = terms_ref[tile].astype(F32)
+        total = pair_ref[group].astype(F32)
         for i, c in enumerate(first):
             c.wait_recv()
             total = total + part_ref[i].astype(F32)
@@ -350,23 +367,27 @@
         total = band_ref[0].astype(F32)
         for b in range(1, bands):
             total = total + band_ref[b].astype(F32)
-        full_ref[tile] = total.astype(BF)
+        full_ref[core, group] = total.astype(BF)
         for c in third:
             c.start()
 
-    def close(total_ref):
+    def swap_back():
         for c in third:
             c.wait_recv()
+        back.start()
+
+    def close(total_ref):
+        back.wait_recv()
         total_ref[...] = full_ref[...]
-        for c in first + second + third:
+        for c in [swap] + first + second + third + [back]:
             c.wait_send()
 
-    return greet, over_lev, gather, close
-
-
-def window_kernel(terms_ref, edge_ref, xh_ref, latent_ref, w2_ref, woutp_ref, gain_ref, wqkv_ref, att_ref, total_ref, vals_ref, pooled_ref, q_ref, kv_ref, part_ref, band_ref, full_ref, send_sem, recv_sem):
+    return greet, over_group, over_lev, gather, swap_back, close
+
+
+def window_kernel(terms_ref, xh_ref, latent_ref, w2_ref, woutp_ref, gain_ref, wqkv_ref, wproj_ref, out_ref, total_ref, vals_ref, pooled_ref, q_ref, kv_ref, att_ref, halves_ref, pair_ref, part_ref, band_ref, full_ref, send_sem, recv_sem):
     gain = gain_ref[...]
-    greet, over_lev, gather, close = sum_stages(terms_ref, part_ref, band_ref, full_ref, send_sem, recv_sem)
+    greet, over_group, over_lev, gather, swap_back, close = sum_stages(terms_ref, halves_ref, pair_ref, part_ref, band_ref, full_ref, send_sem, recv_sem)
     greet()
 
     def halo(group, carry):
@@ -430,9 +451,14 @@
         def _():
             column_rim(0, 2)
             column_rim(1, 3)
+
+        @pl.when(group == 0)
+        def _():
+            over_group()
         return carry
 
     lax.fori_loop(0, 4, halo, 0)
+    over_lev()
 
     def project(rows, column):
         normed = normalise(rows.astype(F32), gain)
@@ -458,7 +484,7 @@
         return carry
 
     lax.fori_loop(1, 4, own, 0)
-    over_lev()
+    gather()
 
     key = lax.broadcasted_iota(jnp.int32, (1, 192), 1)
     odd_lane = lax.broadcasted_iota(jnp.int32, (1, 128), 1) >= HD
@@ -474,9 +500,10 @@
                 expo = jnp.where(valid, expo, 0.0)
             probs = (expo * (1.0 / jnp.sum(expo, axis=-1, keepdims=True))).astype(BF)
             both = dot(probs, kv_ref[window, :, D + pair * 128 : D + pair * 128 + 128])
-            att_ref[column, row0 : row0 + count, lanes] = jnp.where(odd_lane, both[count:], both[:count]).astype(BF)
-
-    inside = (edge_ref[0] == 0, edge_ref[1] == 0)
+            att_ref[row0 : row0 + count, lanes] = jnp.where(odd_lane, both[count:], both[:count]).astype(BF)
+
+    lev = lax.axis_index("lev")
+    inside = (lev > 0, lev < lax.axis_size("lev") - 1)
     plain = [(key < 96) | ok for ok in inside]
     corner = [(key < 48) | ((key < 144) & ((key + 16) % 32 < 16)) | ok for ok in inside]
 
@@ -485,38 +512,39 @@
         attend(0, first, 48 * side, 48, corner[0])
         attend(0, first + 1, 96 + 96 * side, 96, None)
         attend(0, first + 2, 288 + 48 * side, 48, corner[1])
-    gather()
+    back = permutation(384, 1)
+
+    def finish(rows):
+        natural = dot(back, att_ref[...]).astype(BF)
+        return (rows.astype(F32) + dot(natural, wproj_ref[...])).astype(BF)
+
+    done = finish(rows)
+    out_ref[28:32] = done[:192].reshape(4, 3, 16, D)
+    out_ref[0:4] = done[192:].reshape(4, 3, 16, D)
 
     def column_loop(column, carry):
         first = 3 + 3 * column
         attend(column, first, 0, 96, plain[0])
         attend(column, first + 1, 96, 192, None)
         attend(column, first + 2, 288, 96, plain[1])
+        rows = latent_ref[pl.ds(8 * column - 4, 8)].reshape(384, D)
+        out_ref[pl.ds(8 * column - 4, 8)] = finish(rows).reshape(8, 3, 16, D)
+
+        @pl.when(column == 2)
+        def _():
+            swap_back()
+
         return carry
 
     lax.fori_loop(1, 4, column_loop, 0)
     close(total_ref)
 
 
-def finish_kernel(att_ref, latent_ref, wproj_ref, total_ref, we_ref, queries_ref, wkv_ref, out_ref, gembed_ref, gkv_ref, gout_ref, factor):
-    back = permutation(384, 1)
-
-    def finish(column, rows):
-        natural = dot(back, att_ref[column]).astype(BF)
-        return (rows.astype(F32) + dot(natural, wproj_ref[...])).astype(BF)
-
-    rows = jnp.concatenate([latent_ref[28:32].reshape(192, D), latent_ref[0:4].reshape(192, D)], axis=0)
-    done = finish(0, rows)
-    out_ref[28:32] = done[:192].reshape(4, 3, 16, D)
-    out_ref[0:4] = done[192:].reshape(4, 3, 16, D)
-
-    def column_loop(column, carry):
-        rows = latent_ref[pl.ds(8 * column - 4, 8)].reshape(384, D)
-        out_ref[pl.ds(8 * column - 4, 8)] = finish(column, rows).reshape(8, 3, 16, D)
-        return carry
-
-    lax.fori_loop(1, 4, column_loop, 0)
+def finish_kernel(done_ref, total_ref, we_ref, queries_ref, wkv_ref, out_ref, gembed_ref, gkv_ref, gout_ref, sem, factor):
+    copy = pltpu.make_async_copy(done_ref, out_ref, sem)
+    copy.start()
     grads(total_ref, we_ref, queries_ref, wkv_ref, gembed_ref, gkv_ref, gout_ref, factor)
+    copy.wait()
 
 
 def grads(total_ref, we_ref, queries_ref, wkv_ref, gembed_ref, gkv_ref, gout_ref, factor):
@@ -543,20 +571,17 @@
 
 
 def per_device(inputs, level_ids, level_table, w_embed, queries, w_kv, w_out, gain, w_qkv, w_proj, d_latent):
-    band = lax.axis_index("lev")
     bands = lax.axis_size("lev")
     tiles = lax.axis_size("tile")
     lon_rows, lat_rows = d_latent.shape[:2]
-    onehot = (level_ids[:, None] == jnp.arange(level_table.shape[0], dtype=jnp.int32)[None, :]).astype(BF)
-    rows = jnp.dot(onehot, level_table, preferred_element_type=F32).astype(BF)
-    we = jnp.concatenate([w_embed, rows, jnp.zeros((KX - F - LEVELS, D), BF)], axis=0)
+    table = jnp.pad(level_table, ((0, 16 - level_table.shape[0]), (0, 0)))
     vmem = pl.BlockSpec(memory_space=pltpu.VMEM)
     d_nat = d_latent.transpose(0, 2, 1, 3)
-    latent, terms, w2, woutp, far = pl.pallas_call(
+    latent, terms, w2, woutp, far, we = pl.pallas_call(
         pool_kernel,
-        in_specs=[vmem] * 6,
-        out_specs=(vmem,) * 5,
-        out_shape=(whole(d_nat.shape, BF), whole((TERMS, KX), BF), whole((MV, 2 * KX), BF), whole((D, D), BF), whole((LEVELS, F, 512), BF)),
+        in_specs=[pl.BlockSpec(memory_space=pltpu.SMEM)] + [vmem] * 7,
+        out_specs=(vmem,) * 6,
+        out_shape=(whole(d_nat.shape, BF), whole((TERMS, KX), BF), whole((MV, 2 * KX), BF), whole((D, D), BF), whole((LEVELS, F, 512), BF), whole((KX, D), BF)),
         scratch_shapes=[
             pltpu.VMEM((LEVELS, D, 128), F32),
             pltpu.VMEM((D, 384), F32),
@@ -577,36 +602,42 @@
         ],
         compiler_params=params(collective_id=2, has_side_effects=True),
         name="pool",
-    )(inputs[0], d_nat, we, queries, w_kv, w_out)
+    )(level_ids, inputs[0], d_nat, table, w_embed, queries, w_kv, w_out)
 
     factor = 1.0 / math.sqrt(lon_rows * lat_rows * bands * tiles)
-    edge = jnp.stack([band == 0, band == bands - 1]).astype(jnp.int32)
-    att, total = pl.pallas_call(
+    done, total = pl.pallas_call(
         window_kernel,
-        in_specs=[vmem, pl.BlockSpec(memory_space=pltpu.SMEM)] + [vmem] * 6,
+        in_specs=[vmem] * 8,
         out_specs=(vmem, vmem),
-        out_shape=(whole((4, 384, D), BF), whole((16, CHUNK, KX), BF)),
+        out_shape=(whole(d_nat.shape, BF), whole((2, 8, CHUNK, KX), BF)),
         scratch_shapes=[
             pltpu.VMEM((LEVELS, D, 128), F32),
             pltpu.VMEM((D, 384), BF),
             pltpu.VMEM((4, 384, D), BF),
-            pltpu.VMEM((18, 192, 2 * D), BF),
-            pltpu.VMEM((15, CHUNK, KX), BF),
+            pltpu.VMEM((15, 192, 2 * D), BF),
+            pltpu.VMEM((384, D), BF),
             pltpu.VMEM((8, CHUNK, KX), BF),
-            pltpu.VMEM((16, CHUNK, KX), BF),
-            pltpu.SemaphoreType.DMA((37,)),
-            pltpu.SemaphoreType.DMA((37,)),
+            pltpu.VMEM((8, CHUNK, KX), BF),
+            pltpu.VMEM((7, CHUNK, KX), BF),
+            pltpu.VMEM((8, CHUNK, KX), BF),
+            pltpu.VMEM((2, 8, CHUNK, KX), BF),
+            pltpu.SemaphoreType.DMA((23,)),
+            pltpu.SemaphoreType.DMA((23,)),
         ],
         compiler_params=params(collective_id=1, has_side_effects=True),
         name="windows",
-    )(terms.reshape(16, CHUNK, KX), edge, far, latent, w2, woutp, gain.reshape(1, D), w_qkv)
-
+    )(terms.reshape(2, 8, CHUNK, KX), far, latent, w2, woutp, gain.reshape(1, D), w_qkv, w_proj)
+
+    anywhere = pl.BlockSpec(memory_space=pl.ANY)
     out, gembed, gkv, gout = pl.pallas_call(
         functools.partial(finish_kernel, factor=factor),
+        in_specs=[anywhere] + [vmem] * 4,
+        out_specs=(anywhere, vmem, vmem, vmem),
         out_shape=(whole(d_nat.shape, BF), whole((F, D), F32), whole((D, 2 * D), F32), whole((D, D), F32)),
+        scratch_shapes=[pltpu.SemaphoreType.DMA],
         compiler_params=params(),
         name="finish",
-    )(att, latent, w_proj, total.reshape(TERMS, KX), we, queries, w_kv)
+    )(done, total.reshape(TERMS, KX), we, queries, w_kv)
     return (out.transpose(0, 2, 1, 3), gembed, gkv, gout)
 
 

time: 87.9 us -> 125 us (1.42)
  Pallas kernels: 83.8 us -> 123 us
  other arithmetic: 2.23 us -> 0 us
    pallas_call x3, Pallas kernels: 83.8 us -> 123 us  [the longest x1 52 us: per_device(): pl.pallas_call(functools.partial(finish_kernel, factor=factor), in_specs=...]
    concatenate x1 -> x0, other arithmetic: 1.64 us -> none  [per_device(): jnp.concatenate([w_embed, rows, jnp.zeros((KX - F - LEVELS, D), BF)], axi...]
    pad x0 -> x1, local copies, waits for them, and re-layouts: none -> 1.33 us  [per_device(): table = jnp.pad(level_table, ((0, 16 - level_table.shape[0]), (0, 0)))]
where the time goes in v3:
time: 125 us
  Pallas kernels  123 us (98%)
  local copies, waits for them, and re-layouts  1.33 us (1%)
    pallas_call x1, Pallas kernels, per_device(): pl.pallas_call(functools.partial(finish_kernel, factor=factor), in_specs=...  52 us
    pallas_call x1, Pallas kernels, per_device(): pl.pallas_call(window_kernel, in_specs=[vmem] * 8, out_specs=(vmem, vmem)...  38.8 us
    pallas_call x1, Pallas kernels, per_device(): pl.pallas_call(pool_kernel, in_specs=[pl.BlockSpec(memory_space=pltpu.SME...  32 us

profile of v3, /device:TPU:1, one launch (start us, length us, event | category | flops | bytes accessed | tf_op | source)
XLA Modules:
  0.0 124.9 jit_solution(10893958886505989542)
XLA Ops:
  0.6 1.3 %pad.4.table_ref = bf16[16,512]{1,0:T(8,128)(2,1)} pad(bf16[13,512]{1,0:T(8,128)(2,1)} %param.13, bf16[]{:T(256)} %constant.2.clone.1), padding=0_3x0_0 | pad | bytes 29698 | tf_op jit(solution)/shard_map/jit(_pad)/pad | solution.py:577
  2.0 32.0 %pool.1 = (bf16[32,3,16,512]{3,2,1,0:T(8,128)(2,1)}, bf16[2816,128]{1,0:T(8,128)(2,1)}, bf16[544,256]{1,0:T(8,128)(2,1)}, bf16[512,512]{1,0:T(8,128)(2,1)}, bf16...) custom-call(s32[8]{0:T(128)} %ids_ref.1, bf16[80,32,128]{2,1,0:T(8,128)(2,1)} %bitcast.9, ...), custom_call_target="tpu_custom_call" | custom-call | tf_op jit(solution)/shard_map/pool/pallas_call | solution.py:580
  33.9 38.8 %windows.1 = (bf16[32,3,16,512]{3,2,1,0:T(8,128)(2,1)}, bf16[2,8,176,128]{3,2,1,0:T(8,128)(2,1)}) custom-call(bf16[2,8,176,128]{3,2,1,0:T(8,128)(2,1)} %bitcast.8, bf16[8,80,512]{2,1,0:T(8,128)(2,1)} %get-tuple-element.17.xh_ref, bf16[32,3,16,512]{3,2,1,0:T(8,128)(2,1)} %get-tuple-element.18.latent_ref, bf16[544,256]{1,0:T(8,128)(2,1)} %get-tuple-element.19.w2_ref, ...), custom_call_target="tpu_custom_call" | custom-call | tf_op jit(solution)/shard_map/windows/pallas_call | solution.py:608
  72.7 52.0 %finish.1 = (bf16[32,3,16,512]{3,2,1,0:T(8,128)(2,1)}, f32[80,512]{1,0:T(8,128)}, f32[512,1024]{1,0:T(8,128)}, f32[512,512]{1,0:T(8,128)}) custom-call(bf16[32,3,16,512]{3,2,1,0:T(8,128)(2,1)} %get-tuple-element.21.done_ref, bf16[2816,128]{1,0:T(8,128)(2,1)} %bitcast.7, bf16[128,512]{1,0:T(8,128)(2,1)} %get-tuple-element.23.we_ref, ...), custom_call_target="tpu_custom_call" | custom-call | tf_op jit(solution)/shard_map/finish/pallas_call | solution.py:632

commit v4 on v3

--- a/solution.py
+++ b/solution.py
@@ -19,6 +19,7 @@
 KX = 128
 MV = 544
 CHUNK = 176
+UNROLL = 4
 TERMS = 16 * CHUNK
 BF = jnp.bfloat16
 F32 = jnp.float32
@@ -54,11 +55,13 @@
     wanted = jnp.full((16, 1), -1, jnp.int32)
     for l in range(LEVELS):
         wanted = jnp.where(slab == l, ids_ref[l], wanted)
-    onehot = jnp.where(lax.broadcasted_iota(jnp.int32, (16, 16), 1) == wanted, 1.0, 0.0).astype(BF)
+    rows = jnp.zeros((16, D), F32)
+    for entry in range(table_ref.shape[0]):
+        rows = jnp.where(wanted == entry, table_ref[entry : entry + 1, :].astype(F32), rows)
     we_ref[0:F, :] = embed_ref[...]
-    we_ref[F : F + 16, :] = dot(onehot, table_ref[...]).astype(BF)
+    we_ref[F : F + 16, :] = rows.astype(BF)
     we_ref[F + 16 :, :] = jnp.zeros((KX - F - 16, D), BF)
-    row = lax.broadcasted_iota(jnp.int32, (D, D), 0)
+    row = lax.broadcasted_iota(jnp.int32, (D, 1), 0)
     lane = lax.broadcasted_iota(jnp.int32, (D, D), 1)
     mix = jnp.where(lane == (row % HEADS) * HD + row // HEADS, 1.0, 0.0).astype(BF)
     we = we_ref[...]
@@ -125,11 +128,11 @@
 
     own, near, east, west = [], [], [], []
     for off in range(1, bands):
-        own.append(copy(own_ref.at[levs[off]], mine_ref.at[lev], off - 1, place(levs[off], tile)))
-        near.append(copy(near_ref.at[levs[off]], rim_ref.at[lev, :, 256:512], off + 6, place(levs[off], tile)))
+        own.append(lambda g, off=off: copy(own_ref.at[g, levs[off]], mine_ref.at[g, lev], 30 + g * 7 + off - 1, place(levs[off], tile)))
+        near.append(copy(near_ref.at[levs[off]], rim_ref.at[lev, :, 256:512], off - 1, place(levs[off], tile)))
     for off in range(bands):
-        east.append(copy(side_ref.at[0, levs[off]], rim_ref.at[lev, :, 0:128], 14 + off, place(levs[off], next_tile)))
-        west.append(copy(side_ref.at[1, levs[off]], rim_ref.at[lev, :, 128:256], 22 + off, place(levs[off], last_tile)))
+        east.append(copy(side_ref.at[0, levs[off]], rim_ref.at[lev, :, 0:128], 7 + off, place(levs[off], next_tile)))
+        west.append(copy(side_ref.at[1, levs[off]], rim_ref.at[lev, :, 128:256], 15 + off, place(levs[off], last_tile)))
 
     def greet():
         barrier = pltpu.get_barrier_semaphore()
@@ -153,11 +156,13 @@
             out = dot(rows, select(1024, 256, want)).astype(BF)
             for c in range(4):
                 for half in range(2):
-                    own_ref[2 * two + half, :, c * 128 : (c + 1) * 128] = out[c * F : (c + 1) * F, half * 128 : (half + 1) * 128]
+                    own_ref[c, 2 * two + half] = out[c * F : (c + 1) * F, half * 128 : (half + 1) * 128]
         pl.semaphore_wait(pltpu.get_barrier_semaphore(), 3 * bands - 1)
-        for c in own:
-            c.start()
-        mine_ref[lev] = own_ref[lev]
+        for g in range(4):
+            for c in own:
+                c(g).start()
+        for g in range(4):
+            mine_ref[g, lev] = own_ref[g, lev]
 
     def sort_rim():
         rows = xb_ref[...]
@@ -186,16 +191,19 @@
                     side_ref[side, 2 * two + half] = out[side * F : (side + 1) * F, half * 128 : (half + 1) * 128]
         rim_ref[lev, :, 256:512] = near_ref[lev]
 
-    def take_own():
+    def take_own(group):
         for c in own:
-            c.wait_recv()
-        for c in near + east + west:
-            c.start()
+            c(group).wait_recv()
+
+        @pl.when(group == 1)
+        def _():
+            for c in near + east + west:
+                c.start()
 
     def take_rim():
         for c in near + east + west:
             c.wait_recv()
-        for c in own + near + east + west:
+        for c in near + east + west + [c(g) for c in own for g in range(4)]:
             c.wait_send()
 
     return greet, send_own, sort_rim, take_own, take_rim
@@ -209,9 +217,9 @@
     fold_weights(ids_ref, table_ref, embed_ref, queries_ref, wkv_ref, wout_ref, w2_ref, woutp_ref, we_ref)
     tacc_ref[...] = jnp.zeros_like(tacc_ref)
     gacc_ref[...] = jnp.zeros_like(gacc_ref)
-    take_own()
 
     def group_loop(group, carry):
+        take_own(group)
         pool_group(group, mine_ref, d_ref, w2_ref, woutp_ref, latent_ref, vals_ref, dpool_ref, pooled_ref, dv_ref, tacc_ref, gacc_ref)
         return carry
 
@@ -227,8 +235,7 @@
 
 
 def pool_group(group, x_ref, d_ref, w2_ref, woutp_ref, latent_ref, vals_ref, dpool_ref, pooled_ref, dv_ref, tacc_ref, gacc_ref):
-    lane0 = pl.multiple_of(group * 128, 128)
-    pairs, probs = forward_levels(lambda l: x_ref[l, :, pl.ds(lane0, 128)], w2_ref, vals_ref)
+    pairs, probs = forward_levels(lambda l: x_ref[group, l], w2_ref, vals_ref)
     d_rows = jnp.concatenate([d_ref[pl.ds(8 * group, 8), q].reshape(128, D) for q in range(LATENT)], axis=0)
     dpool_ref[...] = dot(woutp_ref[...], d_rows, 1, 1)
     parts = [[probs[l][q * HEADS : (q + 1) * HEADS] for q in range(LATENT)] for l in range(LEVELS)]
@@ -256,7 +263,7 @@
             dv_ref[l // 2, pl.ds(base, 16), lanes] = jnp.concatenate(dvals[l], axis=0).astype(BF)
         return carry
 
-    lax.fori_loop(0, D // 16, mix_loop, 0)
+    lax.fori_loop(0, D // 16, mix_loop, 0, unroll=UNROLL)
 
     def dprob_loop(i, carry):
         acc = list(carry)
@@ -270,7 +277,7 @@
         return tuple(acc)
 
     zero = jnp.zeros((HEADS, 128), F32)
-    dprob = lax.fori_loop(0, D // 16, dprob_loop, (zero,) * (LEVELS * LATENT))
+    dprob = lax.fori_loop(0, D // 16, dprob_loop, (zero,) * (LEVELS * LATENT), unroll=UNROLL)
     scale = 1.0 / math.sqrt(HD)
     delta = []
     for q in range(LATENT):
@@ -303,19 +310,13 @@
     return (centred * lax.rsqrt(var + 1e-05) * gain).astype(BF)
 
 
-def window_index(column, wa):
-    return column * 3 + wa
-
-
-def permutation(rows, dim):
-    dst = lax.broadcasted_iota(jnp.int32, (rows, rows), dim)
-    src = lax.broadcasted_iota(jnp.int32, (rows, rows), 1 - dim)
-    a = dst
-    b = dst - 96
-    c = dst - 288
-    low = (a // 4) * 16 + a % 4
-    mid = (b // 8) * 16 + 4 + b % 8
-    high = (c // 4) * 16 + 12 + c % 4
+def permutation(dim):
+    dst = lax.broadcasted_iota(jnp.int32, (384, 1) if dim == 0 else (1, 384), dim)
+    src = lax.broadcasted_iota(jnp.int32, (384, 384), 1 - dim)
+    mid, high = dst - 96, dst - 288
+    low = (dst // 4) * 16 + dst % 4
+    mid = (mid // 8) * 16 + 4 + mid % 8
+    high = (high // 4) * 16 + 12 + high % 4
     want = jnp.where(dst < 96, low, jnp.where(dst < 288, mid, high))
     return jnp.where(src == want, 1.0, 0.0).astype(BF)
 
@@ -385,10 +386,12 @@
     return greet, over_group, over_lev, gather, swap_back, close
 
 
-def window_kernel(terms_ref, xh_ref, latent_ref, w2_ref, woutp_ref, gain_ref, wqkv_ref, wproj_ref, out_ref, total_ref, vals_ref, pooled_ref, q_ref, kv_ref, att_ref, halves_ref, pair_ref, part_ref, band_ref, full_ref, send_sem, recv_sem):
+def window_kernel(terms_ref, xh_ref, latent_ref, w2_ref, woutp_ref, gain_ref, wqkv_ref, wproj_ref, out_ref, total_ref, vals_ref, pooled_ref, q_ref, kv_ref, att_ref, perm_ref, halves_ref, pair_ref, part_ref, band_ref, full_ref, send_sem, recv_sem):
     gain = gain_ref[...]
     greet, over_group, over_lev, gather, swap_back, close = sum_stages(terms_ref, halves_ref, pair_ref, part_ref, band_ref, full_ref, send_sem, recv_sem)
     greet()
+    perm_ref[0] = permutation(0)
+    perm_ref[1] = permutation(1)
 
     def halo(group, carry):
         lane0 = pl.multiple_of(group * 128, 128)
@@ -412,7 +415,7 @@
                 pooled_ref[pl.ds(base, 16), q * 128 : (q + 1) * 128] = jnp.concatenate(pooled[q], axis=0).astype(BF)
             return inner
 
-        lax.fori_loop(0, D // 16, mix_loop, 0)
+        lax.fori_loop(0, D // 16, mix_loop, 0, unroll=UNROLL)
         latent = dot(pooled_ref[...], woutp_ref[...], 0, 0).astype(BF).astype(F32)
         normed = normalise(latent, gain)
         kv = dot(normed, wqkv_ref[:, D:]).astype(BF)
@@ -462,7 +465,7 @@
 
     def project(rows, column):
         normed = normalise(rows.astype(F32), gain)
-        normed = dot(permutation(384, 0), normed).astype(BF)
+        normed = dot(perm_ref[0], normed).astype(BF)
         q_ref[column] = (dot(normed, wqkv_ref[:, :D]).astype(BF).astype(F32) * (1.0 / math.sqrt(HD))).astype(BF)
         return dot(normed, wqkv_ref[:, D:]).astype(BF)
 
@@ -512,10 +515,9 @@
         attend(0, first, 48 * side, 48, corner[0])
         attend(0, first + 1, 96 + 96 * side, 96, None)
         attend(0, first + 2, 288 + 48 * side, 48, corner[1])
-    back = permutation(384, 1)
 
     def finish(rows):
-        natural = dot(back, att_ref[...]).astype(BF)
+        natural = dot(perm_ref[1], att_ref[...]).astype(BF)
         return (rows.astype(F32) + dot(natural, wproj_ref[...])).astype(BF)
 
     done = finish(rows)
@@ -574,7 +576,6 @@
     bands = lax.axis_size("lev")
     tiles = lax.axis_size("tile")
     lon_rows, lat_rows = d_latent.shape[:2]
-    table = jnp.pad(level_table, ((0, 16 - level_table.shape[0]), (0, 0)))
     vmem = pl.BlockSpec(memory_space=pltpu.VMEM)
     d_nat = d_latent.transpose(0, 2, 1, 3)
     latent, terms, w2, woutp, far, we = pl.pallas_call(
@@ -592,17 +593,17 @@
             pltpu.VMEM((F * 32, 128), F32),
             pltpu.VMEM((4 * F, 1024), BF),
             pltpu.VMEM((4 * F, 1024), BF),
-            pltpu.VMEM((LEVELS, F, 512), BF),
+            pltpu.VMEM((4, LEVELS, F, 128), BF),
             pltpu.VMEM((LEVELS, F, 256), BF),
             pltpu.VMEM((2, LEVELS, F, 128), BF),
+            pltpu.VMEM((4, LEVELS, F, 128), BF),
             pltpu.VMEM((LEVELS, F, 512), BF),
-            pltpu.VMEM((LEVELS, F, 512), BF),
-            pltpu.SemaphoreType.DMA((30,)),
-            pltpu.SemaphoreType.DMA((30,)),
+            pltpu.SemaphoreType.DMA((58,)),
+            pltpu.SemaphoreType.DMA((58,)),
         ],
         compiler_params=params(collective_id=2, has_side_effects=True),
         name="pool",
-    )(level_ids, inputs[0], d_nat, table, w_embed, queries, w_kv, w_out)
+    )(level_ids, inputs[0], d_nat, level_table, w_embed, queries, w_kv, w_out)
 
     factor = 1.0 / math.sqrt(lon_rows * lat_rows * bands * tiles)
     done, total = pl.pallas_call(
@@ -616,6 +617,7 @@
             pltpu.VMEM((4, 384, D), BF),
             pltpu.VMEM((15, 192, 2 * D), BF),
             pltpu.VMEM((384, D), BF),
+            pltpu.VMEM((2, 384, 384), BF),
             pltpu.VMEM((8, CHUNK, KX), BF),
             pltpu.VMEM((8, CHUNK, KX), BF),
             pltpu.VMEM((7, CHUNK, KX), BF),
@@ -631,7 +633,7 @@
     anywhere = pl.BlockSpec(memory_space=pl.ANY)
     out, gembed, gkv, gout = pl.pallas_call(
         functools.partial(finish_kernel, factor=factor),
-        in_specs=[anywhere] + [vmem] * 4,
+        in_specs=[vmem] * 5,
         out_specs=(anywhere, vmem, vmem, vmem),
         out_shape=(whole(d_nat.shape, BF), whole((F, D), F32), whole((D, 2 * D), F32), whole((D, D), F32)),
         scratch_shapes=[pltpu.SemaphoreType.DMA],

time: 125 us -> 72.6 us (0.58)
  Pallas kernels: 123 us -> 71.7 us
  local copies, waits for them, and re-layouts: 1.33 us -> 0 us
    pallas_call x1, Pallas kernels: 52 us -> 5.07 us  [per_device(): pl.pallas_call(functools.partial(finish_kernel, factor=factor), in_specs=...]
    pallas_call x1, Pallas kernels: 32 us -> 29.9 us  [per_device(): pl.pallas_call(pool_kernel, in_specs=[pl.BlockSpec(memory_space=pltpu.SME...]
    pallas_call x1, Pallas kernels: 38.8 us -> 36.7 us  [per_device(): pl.pallas_call(window_kernel, in_specs=[vmem] * 8, out_specs=(vmem, vmem)...]
    pad x1 -> x0, local copies, waits for them, and re-layouts: 1.33 us -> none  [per_device(): table = jnp.pad(level_table, ((0, 16 - level_table.shape[0]), (0, 0)))]
where the time goes in v4:
time: 72.6 us; the launch traced here: 72.5 us
  Pallas kernels  71.7 us (99%)
  between operations  0.81 us (1%)
    pallas_call x1, Pallas kernels, per_device(): pl.pallas_call(window_kernel, in_specs=[vmem] * 8, out_specs=(vmem, vmem)...  36.7 us
    pallas_call x1, Pallas kernels, per_device(): pl.pallas_call(pool_kernel, in_specs=[pl.BlockSpec(memory_space=pltpu.SME...  29.9 us
    pallas_call x1, Pallas kernels, per_device(): pl.pallas_call(functools.partial(finish_kernel, factor=factor), in_specs=...  5.07 us

profile of v4, /device:TPU:1, one launch (start us, length us, event | category | flops | bytes accessed | tf_op | source)
XLA Modules:
  0.0 72.5 jit_solution(14250504503601434123)
XLA Ops:
  0.6 29.9 %pool.1 = (bf16[32,3,16,512]{3,2,1,0:T(8,128)(2,1)}, bf16[2816,128]{1,0:T(8,128)(2,1)}, bf16[544,256]{1,0:T(8,128)(2,1)}, bf16[512,512]{1,0:T(8,128)(2,1)}, bf16...) custom-call(s32[8]{0:T(128)} %ids_ref.1, bf16[80,32,128]{2,1,0:T(8,128)(2,1)} %bitcast.9, ...), custom_call_target="tpu_custom_call" | custom-call | tf_op jit(solution)/shard_map/pool/pallas_call | solution.py:581
  30.5 36.7 %windows.1 = (bf16[32,3,16,512]{3,2,1,0:T(8,128)(2,1)}, bf16[2,8,176,128]{3,2,1,0:T(8,128)(2,1)}) custom-call(bf16[2,8,176,128]{3,2,1,0:T(8,128)(2,1)} %bitcast.8, bf16[8,80,512]{2,1,0:T(8,128)(2,1)} %get-tuple-element.17.xh_ref, bf16[32,3,16,512]{3,2,1,0:T(8,128)(2,1)} %get-tuple-element.18.latent_ref, bf16[544,256]{1,0:T(8,128)(2,1)} %get-tuple-element.19.w2_ref, ...), custom_call_target="tpu_custom_call" | custom-call | tf_op jit(solution)/shard_map/windows/pallas_call | solution.py:609
  67.3 5.1 %finish.1 = (bf16[32,3,16,512]{3,2,1,0:T(8,128)(2,1)}, f32[80,512]{1,0:T(8,128)}, f32[512,1024]{1,0:T(8,128)}, f32[512,512]{1,0:T(8,128)}) custom-call(bf16[32,3,16,512]{3,2,1,0:T(8,128)(2,1)} %get-tuple-element.21.done_ref, bf16[2816,128]{1,0:T(8,128)(2,1)} %bitcast.7, bf16[128,512]{1,0:T(8,128)(2,1)} %get-tuple-element.23.we_ref, ...), custom_call_target="tpu_custom_call" | custom-call | tf_op jit(solution)/shard_map/finish/pallas_call | solution.py:634

commit v5 on v4

--- a/solution.py
+++ b/solution.py
@@ -41,6 +41,13 @@
 
 def remote(src, dst, send, recv, device):
     return pltpu.make_async_remote_copy(src_ref=src, dst_ref=dst, send_sem=send, recv_sem=recv, device_id=device, device_id_type=pl.DeviceIdType.MESH)
+
+
+def fetch(pairs, sems):
+    loads = [pltpu.make_async_copy(src, dst, sems.at[i]) for i, (src, dst) in enumerate(pairs)]
+    for load in loads:
+        load.start()
+    return loads
 
 
 def query_rows(queries):
@@ -209,21 +216,25 @@
     return greet, send_own, sort_rim, take_own, take_rim
 
 
-def pool_kernel(ids_ref, x_ref, d_ref, table_ref, embed_ref, queries_ref, wkv_ref, wout_ref, latent_ref, terms_ref, w2_ref, woutp_ref, far_ref, we_ref, vals_ref, dpool_ref, pooled_ref, dv_ref, tacc_ref, gacc_ref, pixels_ref, xa_ref, xb_ref, own_ref, near_ref, side_ref, mine_ref, rim_ref, send_sem, recv_sem):
+def pool_kernel(ids_ref, x_ref, d_ref, table_ref, embed_ref, queries_ref, wkv_ref, wout_ref, latent_ref, terms_ref, w2_ref, woutp_ref, far_ref, we_ref, vals_ref, dpool_ref, pooled_ref, dv_ref, seen_ref, tacc_ref, gacc_ref, pixels_ref, xa_ref, xb_ref, own_ref, near_ref, side_ref, mine_ref, rim_ref, d_vmem, wkv_vmem, wout_vmem, load_sem, send_sem, recv_sem):
+    loads = fetch(((wkv_ref, wkv_vmem), (wout_ref, wout_vmem), (d_ref, d_vmem)), load_sem)
     greet, send_own, sort_rim, take_own, take_rim = exchange_stages(x_ref, pixels_ref, xa_ref, xb_ref, own_ref, near_ref, side_ref, mine_ref, rim_ref, send_sem, recv_sem)
     greet()
     send_own()
     sort_rim()
-    fold_weights(ids_ref, table_ref, embed_ref, queries_ref, wkv_ref, wout_ref, w2_ref, woutp_ref, we_ref)
-    tacc_ref[...] = jnp.zeros_like(tacc_ref)
+    loads[0].wait()
+    loads[1].wait()
+    fold_weights(ids_ref, table_ref, embed_ref, queries_ref, wkv_vmem, wout_vmem, w2_ref, woutp_ref, we_ref)
     gacc_ref[...] = jnp.zeros_like(gacc_ref)
+    loads[2].wait()
 
     def group_loop(group, carry):
         take_own(group)
-        pool_group(group, mine_ref, d_ref, w2_ref, woutp_ref, latent_ref, vals_ref, dpool_ref, pooled_ref, dv_ref, tacc_ref, gacc_ref)
+        pool_group(group, mine_ref, d_vmem, w2_ref, woutp_ref, latent_ref, vals_ref, dpool_ref, pooled_ref, dv_ref, seen_ref, gacc_ref)
         return carry
 
     lax.fori_loop(0, 4, group_loop, 0)
+    tacc_ref[...] = dot(dv_ref[...], seen_ref[...], 1, 1)
     for h in range(HEADS):
         for j in range(4):
             terms_ref[j * D + h * HD : j * D + (h + 1) * HD, :] = gacc_ref[pl.ds(j * D + h, HD, stride=HEADS), :].astype(BF)
@@ -234,7 +245,8 @@
     far_ref[...] = rim_ref[...]
 
 
-def pool_group(group, x_ref, d_ref, w2_ref, woutp_ref, latent_ref, vals_ref, dpool_ref, pooled_ref, dv_ref, tacc_ref, gacc_ref):
+def pool_group(group, x_ref, d_ref, w2_ref, woutp_ref, latent_ref, vals_ref, dpool_ref, pooled_ref, dv_ref, seen_ref, gacc_ref):
+    column = pl.multiple_of(group * (LEVELS * 128), 128)
     pairs, probs = forward_levels(lambda l: x_ref[group, l], w2_ref, vals_ref)
     d_rows = jnp.concatenate([d_ref[pl.ds(8 * group, 8), q].reshape(128, D) for q in range(LATENT)], axis=0)
     dpool_ref[...] = dot(woutp_ref[...], d_rows, 1, 1)
@@ -259,8 +271,7 @@
         for q in range(LATENT):
             pooled_ref[pl.ds(base, 16), q * 128 : (q + 1) * 128] = jnp.concatenate(pooled[q], axis=0).astype(BF)
         for l in range(LEVELS):
-            lanes = slice((l % 2) * 128, (l % 2) * 128 + 128)
-            dv_ref[l // 2, pl.ds(base, 16), lanes] = jnp.concatenate(dvals[l], axis=0).astype(BF)
+            dv_ref[pl.ds(base, 16), pl.ds(column + l * 128, 128)] = jnp.concatenate(dvals[l], axis=0).astype(BF)
         return carry
 
     lax.fori_loop(0, D // 16, mix_loop, 0, unroll=UNROLL)
@@ -287,13 +298,10 @@
         delta.append(total)
     for l in range(LEVELS):
         ds = [parts[l][q] * (dprob[l * LATENT + q] - delta[q]) * scale for q in range(LATENT)]
-        lanes = slice((l % 2) * 128, (l % 2) * 128 + 128)
-        dv_ref[l // 2, D:MV, lanes] = jnp.concatenate(ds + [zero], axis=0).astype(BF)
-
-    terms = dot(dv_ref[0], pairs[0], 1, 1)
-    for pair in range(1, LEVELS // 2):
-        terms = terms + dot(dv_ref[pair], pairs[pair], 1, 1)
-    tacc_ref[...] += terms
+        dv_ref[D:MV, pl.ds(column + l * 128, 128)] = jnp.concatenate(ds + [zero], axis=0).astype(BF)
+
+    for pair in range(LEVELS // 2):
+        seen_ref[:, pl.ds(column + pair * 256, 256)] = pairs[pair]
     pooled = pooled_ref[...]
     gterm = dot(pooled, d_rows)
     for j in range(4):
@@ -386,12 +394,14 @@
     return greet, over_group, over_lev, gather, swap_back, close
 
 
-def window_kernel(terms_ref, xh_ref, latent_ref, w2_ref, woutp_ref, gain_ref, wqkv_ref, wproj_ref, out_ref, total_ref, vals_ref, pooled_ref, q_ref, kv_ref, att_ref, perm_ref, halves_ref, pair_ref, part_ref, band_ref, full_ref, send_sem, recv_sem):
+def window_kernel(terms_ref, xh_ref, latent_hbm, w2_ref, woutp_ref, gain_ref, wqkv_hbm, wproj_hbm, out_ref, total_ref, vals_ref, pooled_ref, q_ref, kv_ref, att_ref, perm_ref, halves_ref, pair_ref, part_ref, band_ref, full_ref, latent_ref, wqkv_ref, wproj_ref, load_sem, send_sem, recv_sem):
+    loads = fetch(((wqkv_hbm, wqkv_ref), (latent_hbm, latent_ref), (wproj_hbm, wproj_ref)), load_sem)
     gain = gain_ref[...]
     greet, over_group, over_lev, gather, swap_back, close = sum_stages(terms_ref, halves_ref, pair_ref, part_ref, band_ref, full_ref, send_sem, recv_sem)
     greet()
     perm_ref[0] = permutation(0)
     perm_ref[1] = permutation(1)
+    loads[0].wait()
 
     def halo(group, carry):
         lane0 = pl.multiple_of(group * 128, 128)
@@ -462,6 +472,8 @@
 
     lax.fori_loop(0, 4, halo, 0)
     over_lev()
+    loads[1].wait()
+    loads[2].wait()
 
     def project(rows, column):
         normed = normalise(rows.astype(F32), gain)
@@ -490,20 +502,24 @@
     gather()
 
     key = lax.broadcasted_iota(jnp.int32, (1, 192), 1)
+    head_lane = lax.broadcasted_iota(jnp.int32, (1, 256), 1) // HD
     odd_lane = lax.broadcasted_iota(jnp.int32, (1, 128), 1) >= HD
 
     def attend(column, window, row0, count, valid):
-        for pair in range(HEADS // 2):
-            lanes = slice(pair * 128, pair * 128 + 128)
+        for quad in range(HEADS // 4):
+            lanes = slice(quad * 256, quad * 256 + 256)
             q = q_ref[column, row0 : row0 + count, lanes]
             nil = jnp.zeros_like(q)
-            q2 = jnp.concatenate([jnp.where(odd_lane, nil, q), jnp.where(odd_lane, q, nil)], axis=0)
-            expo = jnp.exp(dot(q2, kv_ref[window, :, lanes], 1, 1))
+            q4 = jnp.concatenate([jnp.where(head_lane == h, q, nil) for h in range(4)], axis=0)
+            expo = jnp.exp(dot(q4, kv_ref[window, :, lanes], 1, 1))
             if valid is not None:
                 expo = jnp.where(valid, expo, 0.0)
             probs = (expo * (1.0 / jnp.sum(expo, axis=-1, keepdims=True))).astype(BF)
-            both = dot(probs, kv_ref[window, :, D + pair * 128 : D + pair * 128 + 128])
-            att_ref[row0 : row0 + count, lanes] = jnp.where(odd_lane, both[count:], both[:count]).astype(BF)
+            both = dot(probs, kv_ref[window, :, D + quad * 256 : D + quad * 256 + 256])
+            for two in range(2):
+                part = both[2 * two * count : 2 * (two + 1) * count, two * 128 : (two + 1) * 128]
+                spot = slice(quad * 256 + two * 128, quad * 256 + two * 128 + 128)
+                att_ref[row0 : row0 + count, spot] = jnp.where(odd_lane, part[count:], part[:count]).astype(BF)
 
     lev = lax.axis_index("lev")
     inside = (lev > 0, lev < lax.axis_size("lev") - 1)
@@ -542,26 +558,32 @@
     close(total_ref)
 
 
-def finish_kernel(done_ref, total_ref, we_ref, queries_ref, wkv_ref, out_ref, gembed_ref, gkv_ref, gout_ref, sem, factor):
-    copy = pltpu.make_async_copy(done_ref, out_ref, sem)
-    copy.start()
-    grads(total_ref, we_ref, queries_ref, wkv_ref, gembed_ref, gkv_ref, gout_ref, factor)
-    copy.wait()
-
-
-def grads(total_ref, we_ref, queries_ref, wkv_ref, gembed_ref, gkv_ref, gout_ref, factor):
+def finish_kernel(done_hbm, total_ref, we_ref, queries_ref, wkv_hbm, out_ref, gembed_ref, gkv_ref, gout_ref, done_vmem, wkv_ref, gkv_vmem, gout_vmem, load_sem, save_sem, factor):
+    loads = fetch(((wkv_hbm, wkv_ref), (done_hbm, done_vmem)), load_sem)
+    for j in range(4):
+        gout_vmem[:, j * 128 : (j + 1) * 128] = total_ref[j * D : (j + 1) * D, :].astype(F32) * factor
+    saves = [pltpu.make_async_copy(gout_vmem, gout_ref, save_sem.at[0])]
+    saves[0].start()
     qm = query_rows(queries_ref[...].astype(F32)).astype(BF)
-    for j in range(4):
-        gout_ref[:, j * 128 : (j + 1) * 128] = total_ref[j * D : (j + 1) * D, :].astype(F32) * factor
     values = total_ref[4 * D : 5 * D, :]
     keys = dot(qm, total_ref[5 * D : 5 * D + 32, :][:24], 0, 0)
     khigh, klow = split(keys)
     we = we_ref[...]
-    gkv_ref[:, :D] = (dot(we, khigh, 0, 1) + dot(we, klow, 0, 1)) * factor
-    gkv_ref[:, D:] = dot(we, values, 0, 1) * factor
+    gkv_vmem[1] = dot(we, values, 0, 1) * factor
+    saves.append(pltpu.make_async_copy(gkv_vmem.at[1], gkv_ref.at[:, D : 2 * D], save_sem.at[1]))
+    saves[1].start()
+    gkv_vmem[0] = (dot(we, khigh, 0, 1) + dot(we, klow, 0, 1)) * factor
+    saves.append(pltpu.make_async_copy(gkv_vmem.at[0], gkv_ref.at[:, 0:D], save_sem.at[2]))
+    saves[2].start()
+    loads[0].wait()
+    loads[1].wait()
+    saves.append(pltpu.make_async_copy(done_vmem, out_ref, save_sem.at[3]))
+    saves[3].start()
     wk, wv = wkv_ref[:, :D], wkv_ref[:, D:]
     grad = dot(khigh, wk, 0, 1) + dot(klow, wk, 0, 1) + dot(values, wv, 0, 1)
     gembed_ref[...] = grad[:F] * factor
+    for save in saves:
+        save.wait()
 
 
 def whole(shape, dtype):
@@ -577,17 +599,19 @@
     tiles = lax.axis_size("tile")
     lon_rows, lat_rows = d_latent.shape[:2]
     vmem = pl.BlockSpec(memory_space=pltpu.VMEM)
+    anywhere = pl.BlockSpec(memory_space=pl.ANY)
     d_nat = d_latent.transpose(0, 2, 1, 3)
     latent, terms, w2, woutp, far, we = pl.pallas_call(
         pool_kernel,
-        in_specs=[pl.BlockSpec(memory_space=pltpu.SMEM)] + [vmem] * 7,
+        in_specs=[pl.BlockSpec(memory_space=pltpu.SMEM), vmem, anywhere, vmem, vmem, vmem, anywhere, anywhere],
         out_specs=(vmem,) * 6,
         out_shape=(whole(d_nat.shape, BF), whole((TERMS, KX), BF), whole((MV, 2 * KX), BF), whole((D, D), BF), whole((LEVELS, F, 512), BF), whole((KX, D), BF)),
         scratch_shapes=[
             pltpu.VMEM((LEVELS, D, 128), F32),
             pltpu.VMEM((D, 384), F32),
             pltpu.VMEM((D, 384), BF),
-            pltpu.VMEM((LEVELS // 2, MV, 256), BF),
+            pltpu.VMEM((MV, 4 * LEVELS * 128), BF),
+            pltpu.VMEM((KX, 4 * LEVELS * 128), BF),
             pltpu.VMEM((MV, KX), F32),
             pltpu.VMEM((4 * D, 128), F32),
             pltpu.VMEM((F * 32, 128), F32),
@@ -598,6 +622,10 @@
             pltpu.VMEM((2, LEVELS, F, 128), BF),
             pltpu.VMEM((4, LEVELS, F, 128), BF),
             pltpu.VMEM((LEVELS, F, 512), BF),
+            pltpu.VMEM(d_nat.shape, BF),
+            pltpu.VMEM((D, 2 * D), BF),
+            pltpu.VMEM((D, D), BF),
+            pltpu.SemaphoreType.DMA((3,)),
             pltpu.SemaphoreType.DMA((58,)),
             pltpu.SemaphoreType.DMA((58,)),
         ],
@@ -608,7 +636,7 @@
     factor = 1.0 / math.sqrt(lon_rows * lat_rows * bands * tiles)
     done, total = pl.pallas_call(
         window_kernel,
-        in_specs=[vmem] * 8,
+        in_specs=[vmem, vmem, anywhere, vmem, vmem, vmem, anywhere, anywhere],
         out_specs=(vmem, vmem),
         out_shape=(whole(d_nat.shape, BF), whole((2, 8, CHUNK, KX), BF)),
         scratch_shapes=[
@@ -623,6 +651,10 @@
             pltpu.VMEM((7, CHUNK, KX), BF),
             pltpu.VMEM((8, CHUNK, KX), BF),
             pltpu.VMEM((2, 8, CHUNK, KX), BF),
+            pltpu.VMEM(d_nat.shape, BF),
+            pltpu.VMEM((D, 3 * D), BF),
+            pltpu.VMEM((D, D), BF),
+            pltpu.SemaphoreType.DMA((3,)),
             pltpu.SemaphoreType.DMA((23,)),
             pltpu.SemaphoreType.DMA((23,)),
         ],
@@ -630,13 +662,19 @@
         name="windows",
     )(terms.reshape(2, 8, CHUNK, KX), far, latent, w2, woutp, gain.reshape(1, D), w_qkv, w_proj)
 
-    anywhere = pl.BlockSpec(memory_space=pl.ANY)
     out, gembed, gkv, gout = pl.pallas_call(
         functools.partial(finish_kernel, factor=factor),
-        in_specs=[vmem] * 5,
-        out_specs=(anywhere, vmem, vmem, vmem),
+        in_specs=[anywhere, vmem, vmem, vmem, anywhere],
+        out_specs=(anywhere, vmem, anywhere, anywhere),
         out_shape=(whole(d_nat.shape, BF), whole((F, D), F32), whole((D, 2 * D), F32), whole((D, D), F32)),
-        scratch_shapes=[pltpu.SemaphoreType.DMA],
+        scratch_shapes=[
+            pltpu.VMEM(d_nat.shape, BF),
+            pltpu.VMEM((D, 2 * D), BF),
+            pltpu.VMEM((2, D, D), F32),
+            pltpu.VMEM((D, D), F32),
+            pltpu.SemaphoreType.DMA((2,)),
+            pltpu.SemaphoreType.DMA((4,)),
+        ],
         compiler_params=params(),
         name="finish",
     )(done, total.reshape(TERMS, KX), we, queries, w_kv)

time: 72.6 us -> 69.7 us (0.960)
  Pallas kernels: 71.7 us -> 68.7 us
    pallas_call x1, Pallas kernels: 36.7 us -> 33.4 us  [per_device(): pl.pallas_call(window_kernel, in_specs=[vmem, vmem, anywhere, vmem, vmem,...]
    pallas_call x1, Pallas kernels: 5.07 us -> 6.47 us  [per_device(): pl.pallas_call(functools.partial(finish_kernel, factor=factor), in_specs=...]
    pallas_call x1, Pallas kernels: 29.9 us -> 28.8 us  [per_device(): pl.pallas_call(pool_kernel, in_specs=[pl.BlockSpec(memory_space=pltpu.SME...]
where the time goes in v5:
time: 69.7 us; the launch traced here: 69.5 us
  Pallas kernels  68.7 us (99%)
  between operations  0.81 us (1%)
    pallas_call x1, Pallas kernels, per_device(): pl.pallas_call(window_kernel, in_specs=[vmem, vmem, anywhere, vmem, vmem,...  33.4 us
    pallas_call x1, Pallas kernels, per_device(): pl.pallas_call(pool_kernel, in_specs=[pl.BlockSpec(memory_space=pltpu.SME...  28.8 us
    pallas_call x1, Pallas kernels, per_device(): pl.pallas_call(functools.partial(finish_kernel, factor=factor), in_specs=...  6.47 us

profile of v5, /device:TPU:1, one launch (start us, length us, event | category | flops | bytes accessed | tf_op | source)
XLA Modules:
  0.0 69.5 jit_solution(12152801661399440478)
XLA Ops:
  0.6 28.8 %pool.1 = (bf16[32,3,16,512]{3,2,1,0:T(8,128)(2,1)}, bf16[2816,128]{1,0:T(8,128)(2,1)}, bf16[544,256]{1,0:T(8,128)(2,1)}, bf16[512,512]{1,0:T(8,128)(2,1)}, bf16...) custom-call(s32[8]{0:T(128)} %ids_ref.1, bf16[80,32,128]{2,1,0:T(8,128)(2,1)} %bitcast.9, ...), custom_call_target="tpu_custom_call" | custom-call | tf_op jit(solution)/shard_map/pool/pallas_call | solution.py:604
  29.4 33.4 %windows.1 = (bf16[32,3,16,512]{3,2,1,0:T(8,128)(2,1)}, bf16[2,8,176,128]{3,2,1,0:T(8,128)(2,1)}) custom-call(bf16[2,8,176,128]{3,2,1,0:T(8,128)(2,1)} %bitcast.8, bf16[8,80,512]{2,1,0:T(8,128)(2,1)} %get-tuple-element.17.xh_ref, bf16[32,3,16,512]{3,2,1,0:T(8,128)(2,1)} %get-tuple-element.18.latent_hbm, bf16[544,256]{1,0:T(8,128)(2,1)} %get-tuple-element.19.w2_ref, ...), custom_call_target="tpu_custom_call" | custom-call | tf_op jit(solution)/shard_map/windows/pallas_call | solution.py:637
  62.8 6.5 %finish.1 = (bf16[32,3,16,512]{3,2,1,0:T(8,128)(2,1)}, f32[80,512]{1,0:T(8,128)}, f32[512,1024]{1,0:T(8,128)}, f32[512,512]{1,0:T(8,128)}) custom-call(bf16[32,3,16,512]{3,2,1,0:T(8,128)(2,1)} %get-tuple-element.21.done_hbm, bf16[2816,128]{1,0:T(8,128)(2,1)} %bitcast.7, bf16[128,512]{1,0:T(8,128)(2,1)} %get-tuple-element.23.we_ref, ...), custom_call_target="tpu_custom_call" | custom-call | tf_op jit(solution)/shard_map/finish/pallas_call | solution.py:665

commit v6 on v5

--- a/solution.py
+++ b/solution.py
@@ -329,54 +329,57 @@
     return jnp.where(src == want, 1.0, 0.0).astype(BF)
 
 
-def sum_stages(terms_ref, halves_ref, pair_ref, part_ref, band_ref, full_ref, send_sem, recv_sem):
+def sum_stages(start, size, slot0, terms_ref, halves_ref, pair_ref, part_ref, band_ref, full_ref, send_sem, recv_sem):
+    cut = pl.ds(start, size)
     lev, tile = lax.axis_index("lev"), lax.axis_index("tile")
     bands, tiles = lax.axis_size("lev"), lax.axis_size("tile")
     groups = tiles // 2
     group, core = tile // 2, lax.rem(tile, 2)
 
     def copy(src, dst, slot, device):
-        return remote(src, dst, send_sem.at[slot], recv_sem.at[slot], device)
+        return remote(src, dst, send_sem.at[slot0 + slot], recv_sem.at[slot0 + slot], device)
 
     other = place(lev, 2 * group + 1 - core)
     lev_peers = [place(lax.rem(lev + off, bands), tile) for off in range(1, bands)]
     group_ids = [lax.rem(group + off, groups) for off in range(1, groups)]
     group_peers = [place(lev, 2 * g + core) for g in group_ids]
-    swap = copy(terms_ref.at[1 - core], halves_ref, 0, other)
-    first = [copy(pair_ref.at[g], part_ref.at[i], 1 + i, group_peers[i]) for i, g in enumerate(group_ids)]
-    second = [copy(band_ref.at[lev], band_ref.at[lev], 8 + i, peer) for i, peer in enumerate(lev_peers)]
-    third = [copy(full_ref.at[core, group], full_ref.at[core, group], 15 + i, peer) for i, peer in enumerate(group_peers)]
-    back = copy(full_ref.at[core], full_ref.at[core], 22, other)
+    swap = copy(terms_ref.at[1 - core, :, cut, :], halves_ref.at[:, cut, :], 0, other)
+    first = [copy(pair_ref.at[g, cut, :], part_ref.at[i, cut, :], 1 + i, group_peers[i]) for i, g in enumerate(group_ids)]
+    second = [copy(band_ref.at[lev, cut, :], band_ref.at[lev, cut, :], 8 + i, peer) for i, peer in enumerate(lev_peers)]
+    third = [copy(full_ref.at[core, group, cut, :], full_ref.at[core, group, cut, :], 15 + i, peer) for i, peer in enumerate(group_peers)]
+    back = copy(full_ref.at[core, :, cut, :], full_ref.at[core, :, cut, :], 22, other)
 
     def greet():
         barrier = pltpu.get_barrier_semaphore()
         for peer in group_peers + lev_peers + [other]:
             pl.semaphore_signal(barrier, inc=1, device_id=peer, device_id_type=pl.DeviceIdType.MESH)
         pl.semaphore_wait(barrier, groups + bands - 1)
+
+    def begin():
         swap.start()
 
     def over_group():
         swap.wait_recv()
-        pair_ref[...] = (terms_ref[core].astype(F32) + halves_ref[...].astype(F32)).astype(BF)
+        pair_ref[:, cut, :] = (terms_ref[core, :, cut, :].astype(F32) + halves_ref[:, cut, :].astype(F32)).astype(BF)
         for c in first:
             c.start()
 
     def over_lev():
-        total = pair_ref[group].astype(F32)
+        total = pair_ref[group, cut, :].astype(F32)
         for i, c in enumerate(first):
             c.wait_recv()
-            total = total + part_ref[i].astype(F32)
-        band_ref[lev] = total.astype(BF)
+            total = total + part_ref[i, cut, :].astype(F32)
+        band_ref[lev, cut, :] = total.astype(BF)
         for c in second:
             c.start()
 
     def gather():
         for c in second:
             c.wait_recv()
-        total = band_ref[0].astype(F32)
+        total = band_ref[0, cut, :].astype(F32)
         for b in range(1, bands):
-            total = total + band_ref[b].astype(F32)
-        full_ref[core, group] = total.astype(BF)
+            total = total + band_ref[b, cut, :].astype(F32)
+        full_ref[core, group, cut, :] = total.astype(BF)
         for c in third:
             c.start()
 
@@ -387,18 +390,22 @@
 
     def close(total_ref):
         back.wait_recv()
-        total_ref[...] = full_ref[...]
+        total_ref[:, :, cut, :] = full_ref[:, :, cut, :]
         for c in [swap] + first + second + third + [back]:
             c.wait_send()
 
-    return greet, over_group, over_lev, gather, swap_back, close
+    return greet, begin, over_group, over_lev, gather, swap_back, close
 
 
 def window_kernel(terms_ref, xh_ref, latent_hbm, w2_ref, woutp_ref, gain_ref, wqkv_hbm, wproj_hbm, out_ref, total_ref, vals_ref, pooled_ref, q_ref, kv_ref, att_ref, perm_ref, halves_ref, pair_ref, part_ref, band_ref, full_ref, latent_ref, wqkv_ref, wproj_ref, load_sem, send_sem, recv_sem):
     loads = fetch(((wqkv_hbm, wqkv_ref), (latent_hbm, latent_ref), (wproj_hbm, wproj_ref)), load_sem)
     gain = gain_ref[...]
-    greet, over_group, over_lev, gather, swap_back, close = sum_stages(terms_ref, halves_ref, pair_ref, part_ref, band_ref, full_ref, send_sem, recv_sem)
+    buffers = (terms_ref, halves_ref, pair_ref, part_ref, band_ref, full_ref, send_sem, recv_sem)
+    greet, begin_a, over_group_a, over_lev_a, gather_a, swap_back_a, close_a = sum_stages(0, 96, 0, *buffers)
+    _, begin_b, over_group_b, over_lev_b, gather_b, swap_back_b, close_b = sum_stages(96, CHUNK - 96, 23, *buffers)
     greet()
+    begin_a()
+    begin_b()
     perm_ref[0] = permutation(0)
     perm_ref[1] = permutation(1)
     loads[0].wait()
@@ -467,11 +474,12 @@
 
         @pl.when(group == 0)
         def _():
-            over_group()
+            over_group_a()
+            over_group_b()
         return carry
 
     lax.fori_loop(0, 4, halo, 0)
-    over_lev()
+    over_lev_a()
     loads[1].wait()
     loads[2].wait()
 
@@ -489,6 +497,8 @@
         kv_ref[first + 1, 0:96, :] = kv[96 + 96 * side : 192 + 96 * side]
         kv_ref[first + 2, 0:48, :] = kv[288 + 48 * side : 336 + 48 * side]
 
+    over_lev_b()
+
     def own(column, carry):
         rows = latent_ref[pl.ds(8 * column - 4, 8)].reshape(384, D)
         kv = project(rows, column)
@@ -496,10 +506,15 @@
         kv_ref[first, 0:96, :] = kv[0:96]
         kv_ref[first + 1, 0:192, :] = kv[96:288]
         kv_ref[first + 2, 0:96, :] = kv[288:384]
+
+        @pl.when(column == 2)
+        def _():
+            gather_a()
+
         return carry
 
     lax.fori_loop(1, 4, own, 0)
-    gather()
+    gather_b()
 
     key = lax.broadcasted_iota(jnp.int32, (1, 192), 1)
     head_lane = lax.broadcasted_iota(jnp.int32, (1, 256), 1) // HD
@@ -539,6 +554,7 @@
     done = finish(rows)
     out_ref[28:32] = done[:192].reshape(4, 3, 16, D)
     out_ref[0:4] = done[192:].reshape(4, 3, 16, D)
+    swap_back_a()
 
     def column_loop(column, carry):
         first = 3 + 3 * column
@@ -550,35 +566,33 @@
 
         @pl.when(column == 2)
         def _():
-            swap_back()
+            swap_back_b()
 
         return carry
 
     lax.fori_loop(1, 4, column_loop, 0)
-    close(total_ref)
+    close_a(total_ref)
+    close_b(total_ref)
 
 
 def finish_kernel(done_hbm, total_ref, we_ref, queries_ref, wkv_hbm, out_ref, gembed_ref, gkv_ref, gout_ref, done_vmem, wkv_ref, gkv_vmem, gout_vmem, load_sem, save_sem, factor):
-    loads = fetch(((wkv_hbm, wkv_ref), (done_hbm, done_vmem)), load_sem)
+    blocks = [pl.ds(8 * i, 8) for i in range(4)]
+    loads = fetch([(done_hbm.at[block], done_vmem.at[block]) for block in blocks] + [(wkv_hbm, wkv_ref)], load_sem)
     for j in range(4):
         gout_vmem[:, j * 128 : (j + 1) * 128] = total_ref[j * D : (j + 1) * D, :].astype(F32) * factor
-    saves = [pltpu.make_async_copy(gout_vmem, gout_ref, save_sem.at[0])]
-    saves[0].start()
+    saves = fetch([(gout_vmem, gout_ref)], save_sem.at[pl.ds(5, 1)])
+    for load in loads[:4]:
+        load.wait()
+    saves += fetch([(done_vmem.at[block], out_ref.at[block]) for block in blocks], save_sem)
     qm = query_rows(queries_ref[...].astype(F32)).astype(BF)
     values = total_ref[4 * D : 5 * D, :]
     keys = dot(qm, total_ref[5 * D : 5 * D + 32, :][:24], 0, 0)
     khigh, klow = split(keys)
     we = we_ref[...]
-    gkv_vmem[1] = dot(we, values, 0, 1) * factor
-    saves.append(pltpu.make_async_copy(gkv_vmem.at[1], gkv_ref.at[:, D : 2 * D], save_sem.at[1]))
-    saves[1].start()
-    gkv_vmem[0] = (dot(we, khigh, 0, 1) + dot(we, klow, 0, 1)) * factor
-    saves.append(pltpu.make_async_copy(gkv_vmem.at[0], gkv_ref.at[:, 0:D], save_sem.at[2]))
-    saves[2].start()
-    loads[0].wait()
-    loads[1].wait()
-    saves.append(pltpu.make_async_copy(done_vmem, out_ref, save_sem.at[3]))
-    saves[3].start()
+    gkv_vmem[:, D:] = dot(we, values, 0, 1) * factor
+    gkv_vmem[:, :D] = (dot(we, khigh, 0, 1) + dot(we, klow, 0, 1)) * factor
+    saves += fetch([(gkv_vmem, gkv_ref)], save_sem.at[pl.ds(4, 1)])
+    loads[4].wait()
     wk, wv = wkv_ref[:, :D], wkv_ref[:, D:]
     grad = dot(khigh, wk, 0, 1) + dot(klow, wk, 0, 1) + dot(values, wv, 0, 1)
     gembed_ref[...] = grad[:F] * factor
@@ -655,8 +669,8 @@
             pltpu.VMEM((D, 3 * D), BF),
             pltpu.VMEM((D, D), BF),
             pltpu.SemaphoreType.DMA((3,)),
-            pltpu.SemaphoreType.DMA((23,)),
-            pltpu.SemaphoreType.DMA((23,)),
+            pltpu.SemaphoreType.DMA((46,)),
+            pltpu.SemaphoreType.DMA((46,)),
         ],
         compiler_params=params(collective_id=1, has_side_effects=True),
         name="windows",
@@ -670,10 +684,10 @@
         scratch_shapes=[
             pltpu.VMEM(d_nat.shape, BF),
             pltpu.VMEM((D, 2 * D), BF),
-            pltpu.VMEM((2, D, D), F32),
+            pltpu.VMEM((D, 2 * D), F32),
             pltpu.VMEM((D, D), F32),
-            pltpu.SemaphoreType.DMA((2,)),
-            pltpu.SemaphoreType.DMA((4,)),
+            pltpu.SemaphoreType.DMA((5,)),
+            pltpu.SemaphoreType.DMA((6,)),
         ],
         compiler_params=params(),
         name="finish",

time: 69.7 us -> 69.9 us (level)
    pallas_call x1, Pallas kernels: 33.4 us -> 34.5 us  [per_device(): pl.pallas_call(window_kernel, in_specs=[vmem, vmem, anywhere, vmem, vmem,...]
    pallas_call x1, Pallas kernels: 6.47 us -> 5.64 us  [per_device(): pl.pallas_call(functools.partial(finish_kernel, factor=factor), in_specs=...]
where the time goes in v6:
time: 69.9 us; the launch traced here: 69.7 us
  Pallas kernels  68.9 us (99%)
  between operations  0.81 us (1%)
    pallas_call x1, Pallas kernels, per_device(): pl.pallas_call(window_kernel, in_specs=[vmem, vmem, anywhere, vmem, vmem,...  34.5 us
    pallas_call x1, Pallas kernels, per_device(): pl.pallas_call(pool_kernel, in_specs=[pl.BlockSpec(memory_space=pltpu.SME...  28.8 us
    pallas_call x1, Pallas kernels, per_device(): pl.pallas_call(functools.partial(finish_kernel, factor=factor), in_specs=...  5.64 us

profile of v6, /device:TPU:1, one launch (start us, length us, event | category | flops | bytes accessed | tf_op | source)
XLA Modules:
  0.0 69.7 jit_solution(17786658944818719067)
XLA Ops:
  0.6 28.8 %pool.1 = (bf16[32,3,16,512]{3,2,1,0:T(8,128)(2,1)}, bf16[2816,128]{1,0:T(8,128)(2,1)}, bf16[544,256]{1,0:T(8,128)(2,1)}, bf16[512,512]{1,0:T(8,128)(2,1)}, bf16...) custom-call(s32[8]{0:T(128)} %ids_ref.1, bf16[80,32,128]{2,1,0:T(8,128)(2,1)} %bitcast.9, ...), custom_call_target="tpu_custom_call" | custom-call | tf_op jit(solution)/shard_map/pool/pallas_call | solution.py:618
  29.4 34.5 %windows.1 = (bf16[32,3,16,512]{3,2,1,0:T(8,128)(2,1)}, bf16[2,8,176,128]{3,2,1,0:T(8,128)(2,1)}) custom-call(bf16[2,8,176,128]{3,2,1,0:T(8,128)(2,1)} %bitcast.8, bf16[8,80,512]{2,1,0:T(8,128)(2,1)} %get-tuple-element.17.xh_ref, bf16[32,3,16,512]{3,2,1,0:T(8,128)(2,1)} %get-tuple-element.18.latent_hbm, bf16[544,256]{1,0:T(8,128)(2,1)} %get-tuple-element.19.w2_ref, ...), custom_call_target="tpu_custom_call" | custom-call | tf_op jit(solution)/shard_map/windows/pallas_call | solution.py:651
  63.9 5.6 %finish.1 = (bf16[32,3,16,512]{3,2,1,0:T(8,128)(2,1)}, f32[80,512]{1,0:T(8,128)}, f32[512,1024]{1,0:T(8,128)}, f32[512,512]{1,0:T(8,128)}) custom-call(bf16[32,3,16,512]{3,2,1,0:T(8,128)(2,1)} %get-tuple-element.21.done_hbm, bf16[2816,128]{1,0:T(8,128)(2,1)} %bitcast.7, bf16[128,512]{1,0:T(8,128)(2,1)} %get-tuple-element.23.we_ref, ...), custom_call_target="tpu_custom_call" | custom-call | tf_op jit(solution)/shard_map/finish/pallas_call | solution.py:679

commit v7 on v6

--- a/solution.py
+++ b/solution.py
@@ -475,11 +475,14 @@
         @pl.when(group == 0)
         def _():
             over_group_a()
+
+        @pl.when(group == 2)
+        def _():
+            over_lev_a()
             over_group_b()
         return carry
 
     lax.fori_loop(0, 4, halo, 0)
-    over_lev_a()
     loads[1].wait()
     loads[2].wait()
 
@@ -497,6 +500,7 @@
         kv_ref[first + 1, 0:96, :] = kv[96 + 96 * side : 192 + 96 * side]
         kv_ref[first + 2, 0:48, :] = kv[288 + 48 * side : 336 + 48 * side]
 
+    gather_a()
     over_lev_b()
 
     def own(column, carry):
@@ -506,14 +510,10 @@
         kv_ref[first, 0:96, :] = kv[0:96]
         kv_ref[first + 1, 0:192, :] = kv[96:288]
         kv_ref[first + 2, 0:96, :] = kv[288:384]
-
-        @pl.when(column == 2)
-        def _():
-            gather_a()
-
         return carry
 
     lax.fori_loop(1, 4, own, 0)
+    swap_back_a()
     gather_b()
 
     key = lax.broadcasted_iota(jnp.int32, (1, 192), 1)
@@ -554,7 +554,6 @@
     done = finish(rows)
     out_ref[28:32] = done[:192].reshape(4, 3, 16, D)
     out_ref[0:4] = done[192:].reshape(4, 3, 16, D)
-    swap_back_a()
 
     def column_loop(column, carry):
         first = 3 + 3 * column
@@ -564,7 +563,7 @@
         rows = latent_ref[pl.ds(8 * column - 4, 8)].reshape(384, D)
         out_ref[pl.ds(8 * column - 4, 8)] = finish(rows).reshape(8, 3, 16, D)
 
-        @pl.when(column == 2)
+        @pl.when(column == 1)
         def _():
             swap_back_b()
 
@@ -575,29 +574,21 @@
     close_b(total_ref)
 
 
-def finish_kernel(done_hbm, total_ref, we_ref, queries_ref, wkv_hbm, out_ref, gembed_ref, gkv_ref, gout_ref, done_vmem, wkv_ref, gkv_vmem, gout_vmem, load_sem, save_sem, factor):
-    blocks = [pl.ds(8 * i, 8) for i in range(4)]
-    loads = fetch([(done_hbm.at[block], done_vmem.at[block]) for block in blocks] + [(wkv_hbm, wkv_ref)], load_sem)
+def finish_kernel(done_ref, total_ref, we_ref, queries_ref, wkv_ref, out_ref, gembed_ref, gkv_ref, gout_ref, save_sem, factor):
+    saves = fetch([(done_ref, out_ref)], save_sem)
     for j in range(4):
-        gout_vmem[:, j * 128 : (j + 1) * 128] = total_ref[j * D : (j + 1) * D, :].astype(F32) * factor
-    saves = fetch([(gout_vmem, gout_ref)], save_sem.at[pl.ds(5, 1)])
-    for load in loads[:4]:
-        load.wait()
-    saves += fetch([(done_vmem.at[block], out_ref.at[block]) for block in blocks], save_sem)
+        gout_ref[:, j * 128 : (j + 1) * 128] = total_ref[j * D : (j + 1) * D, :].astype(F32) * factor
     qm = query_rows(queries_ref[...].astype(F32)).astype(BF)
     values = total_ref[4 * D : 5 * D, :]
     keys = dot(qm, total_ref[5 * D : 5 * D + 32, :][:24], 0, 0)
     khigh, klow = split(keys)
     we = we_ref[...]
-    gkv_vmem[:, D:] = dot(we, values, 0, 1) * factor
-    gkv_vmem[:, :D] = (dot(we, khigh, 0, 1) + dot(we, klow, 0, 1)) * factor
-    saves += fetch([(gkv_vmem, gkv_ref)], save_sem.at[pl.ds(4, 1)])
-    loads[4].wait()
+    gkv_ref[:, D:] = dot(we, values, 0, 1) * factor
+    gkv_ref[:, :D] = (dot(we, khigh, 0, 1) + dot(we, klow, 0, 1)) * factor
     wk, wv = wkv_ref[:, :D], wkv_ref[:, D:]
     grad = dot(khigh, wk, 0, 1) + dot(klow, wk, 0, 1) + dot(values, wv, 0, 1)
     gembed_ref[...] = grad[:F] * factor
-    for save in saves:
-        save.wait()
+    saves[0].wait()
 
 
 def whole(shape, dtype):
@@ -678,17 +669,10 @@
 
     out, gembed, gkv, gout = pl.pallas_call(
         functools.partial(finish_kernel, factor=factor),
-        in_specs=[anywhere, vmem, vmem, vmem, anywhere],
-        out_specs=(anywhere, vmem, anywhere, anywhere),
+        in_specs=[vmem] * 5,
+        out_specs=(anywhere, vmem, vmem, vmem),
         out_shape=(whole(d_nat.shape, BF), whole((F, D), F32), whole((D, 2 * D), F32), whole((D, D), F32)),
-        scratch_shapes=[
-            pltpu.VMEM(d_nat.shape, BF),
-            pltpu.VMEM((D, 2 * D), BF),
-            pltpu.VMEM((D, 2 * D), F32),
-            pltpu.VMEM((D, D), F32),
-            pltpu.SemaphoreType.DMA((5,)),
-            pltpu.SemaphoreType.DMA((6,)),
-        ],
+        scratch_shapes=[pltpu.SemaphoreType.DMA((1,))],
         compiler_params=params(),
         name="finish",
     )(done, total.reshape(TERMS, KX), we, queries, w_kv)

time: 69.9 us -> 71.7 us (1.026)
  Pallas kernels: 68.9 us -> 70 us
    pallas_call x1, Pallas kernels: 34.5 us -> 36.3 us  [per_device(): pl.pallas_call(window_kernel, in_specs=[vmem, vmem, anywhere, vmem, vmem,...]
where the time goes in v7:
time: 71.7 us; the launch traced here: 70.8 us
  Pallas kernels  70 us (98%)
  between operations  0.81 us (1%)
    pallas_call x1, Pallas kernels, per_device(): pl.pallas_call(window_kernel, in_specs=[vmem, vmem, anywhere, vmem, vmem,...  36.3 us
    pallas_call x1, Pallas kernels, per_device(): pl.pallas_call(pool_kernel, in_specs=[pl.BlockSpec(memory_space=pltpu.SME...  28.8 us
    pallas_call x1, Pallas kernels, per_device(): pl.pallas_call(functools.partial(finish_kernel, factor=factor), in_specs=...  4.93 us

profile of v7, /device:TPU:1, one launch (start us, length us, event | category | flops | bytes accessed | tf_op | source)
XLA Modules:
  0.0 70.8 jit_solution(10973219121538450655)
XLA Ops:
  0.6 28.8 %pool.1 = (bf16[32,3,16,512]{3,2,1,0:T(8,128)(2,1)}, bf16[2816,128]{1,0:T(8,128)(2,1)}, bf16[544,256]{1,0:T(8,128)(2,1)}, bf16[512,512]{1,0:T(8,128)(2,1)}, bf16...) custom-call(s32[8]{0:T(128)} %ids_ref.1, bf16[80,32,128]{2,1,0:T(8,128)(2,1)} %bitcast.9, ...), custom_call_target="tpu_custom_call" | custom-call | tf_op jit(solution)/shard_map/pool/pallas_call | solution.py:609
  29.4 36.3 %windows.1 = (bf16[32,3,16,512]{3,2,1,0:T(8,128)(2,1)}, bf16[2,8,176,128]{3,2,1,0:T(8,128)(2,1)}) custom-call(bf16[2,8,176,128]{3,2,1,0:T(8,128)(2,1)} %bitcast.8, bf16[8,80,512]{2,1,0:T(8,128)(2,1)} %get-tuple-element.17.xh_ref, bf16[32,3,16,512]{3,2,1,0:T(8,128)(2,1)} %get-tuple-element.18.latent_hbm, bf16[544,256]{1,0:T(8,128)(2,1)} %get-tuple-element.19.w2_ref, ...), custom_call_target="tpu_custom_call" | custom-call | tf_op jit(solution)/shard_map/windows/pallas_call | solution.py:642
  65.7 4.9 %finish.1 = (bf16[32,3,16,512]{3,2,1,0:T(8,128)(2,1)}, f32[80,512]{1,0:T(8,128)}, f32[512,1024]{1,0:T(8,128)}, f32[512,512]{1,0:T(8,128)}) custom-call(bf16[32,3,16,512]{3,2,1,0:T(8,128)(2,1)} %get-tuple-element.21.done_ref, bf16[2816,128]{1,0:T(8,128)(2,1)} %bitcast.7, bf16[128,512]{1,0:T(8,128)(2,1)} %get-tuple-element.23.we_ref, ...), custom_call_target="tpu_custom_call" | custom-call | tf_op jit(solution)/shard_map/finish/pallas_call | solution.py:670

commit v8 on v5

--- a/solution.py
+++ b/solution.py
@@ -558,32 +558,21 @@
     close(total_ref)
 
 
-def finish_kernel(done_hbm, total_ref, we_ref, queries_ref, wkv_hbm, out_ref, gembed_ref, gkv_ref, gout_ref, done_vmem, wkv_ref, gkv_vmem, gout_vmem, load_sem, save_sem, factor):
-    loads = fetch(((wkv_hbm, wkv_ref), (done_hbm, done_vmem)), load_sem)
+def finish_kernel(done_ref, total_ref, we_ref, queries_ref, wkv_ref, out_ref, gembed_ref, gkv_ref, gout_ref, save_sem, factor):
+    saves = fetch([(done_ref, out_ref)], save_sem)
     for j in range(4):
-        gout_vmem[:, j * 128 : (j + 1) * 128] = total_ref[j * D : (j + 1) * D, :].astype(F32) * factor
-    saves = [pltpu.make_async_copy(gout_vmem, gout_ref, save_sem.at[0])]
-    saves[0].start()
+        gout_ref[:, j * 128 : (j + 1) * 128] = total_ref[j * D : (j + 1) * D, :].astype(F32) * factor
     qm = query_rows(queries_ref[...].astype(F32)).astype(BF)
     values = total_ref[4 * D : 5 * D, :]
     keys = dot(qm, total_ref[5 * D : 5 * D + 32, :][:24], 0, 0)
     khigh, klow = split(keys)
     we = we_ref[...]
-    gkv_vmem[1] = dot(we, values, 0, 1) * factor
-    saves.append(pltpu.make_async_copy(gkv_vmem.at[1], gkv_ref.at[:, D : 2 * D], save_sem.at[1]))
-    saves[1].start()
-    gkv_vmem[0] = (dot(we, khigh, 0, 1) + dot(we, klow, 0, 1)) * factor
-    saves.append(pltpu.make_async_copy(gkv_vmem.at[0], gkv_ref.at[:, 0:D], save_sem.at[2]))
-    saves[2].start()
-    loads[0].wait()
-    loads[1].wait()
-    saves.append(pltpu.make_async_copy(done_vmem, out_ref, save_sem.at[3]))
-    saves[3].start()
+    gkv_ref[:, D:] = dot(we, values, 0, 1) * factor
+    gkv_ref[:, :D] = (dot(we, khigh, 0, 1) + dot(we, klow, 0, 1)) * factor
     wk, wv = wkv_ref[:, :D], wkv_ref[:, D:]
     grad = dot(khigh, wk, 0, 1) + dot(klow, wk, 0, 1) + dot(values, wv, 0, 1)
     gembed_ref[...] = grad[:F] * factor
-    for save in saves:
-        save.wait()
+    saves[0].wait()
 
 
 def whole(shape, dtype):
@@ -664,17 +653,10 @@
 
     out, gembed, gkv, gout = pl.pallas_call(
         functools.partial(finish_kernel, factor=factor),
-        in_specs=[anywhere, vmem, vmem, vmem, anywhere],
-        out_specs=(anywhere, vmem, anywhere, anywhere),
+        in_specs=[vmem] * 5,
+        out_specs=(anywhere, vmem, vmem, vmem),
         out_shape=(whole(d_nat.shape, BF), whole((F, D), F32), whole((D, 2 * D), F32), whole((D, D), F32)),
-        scratch_shapes=[
-            pltpu.VMEM(d_nat.shape, BF),
-            pltpu.VMEM((D, 2 * D), BF),
-            pltpu.VMEM((2, D, D), F32),
-            pltpu.VMEM((D, D), F32),
-            pltpu.SemaphoreType.DMA((2,)),
-            pltpu.SemaphoreType.DMA((4,)),
-        ],
+        scratch_shapes=[pltpu.SemaphoreType.DMA((1,))],
         compiler_params=params(),
         name="finish",
     )(done, total.reshape(TERMS, KX), we, queries, w_kv)

time: 69.7 us -> 68.1 us (0.977)
  Pallas kernels: 68.7 us -> 67.1 us
    pallas_call x1, Pallas kernels: 6.47 us -> 4.93 us  [per_device(): pl.pallas_call(functools.partial(finish_kernel, factor=factor), in_specs=...]
where the time goes in v8:
time: 68.1 us; the launch traced here: 67.9 us
  Pallas kernels  67.1 us (99%)
  between operations  0.81 us (1%)
    pallas_call x1, Pallas kernels, per_device(): pl.pallas_call(window_kernel, in_specs=[vmem, vmem, anywhere, vmem, vmem,...  33.4 us
    pallas_call x1, Pallas kernels, per_device(): pl.pallas_call(pool_kernel, in_specs=[pl.BlockSpec(memory_space=pltpu.SME...  28.8 us
    pallas_call x1, Pallas kernels, per_device(): pl.pallas_call(functools.partial(finish_kernel, factor=factor), in_specs=...  4.93 us

profile of v8, /device:TPU:1, one launch (start us, length us, event | category | flops | bytes accessed | tf_op | source)
XLA Modules:
  0.0 67.9 jit_solution(10886713967315549877)
XLA Ops:
  0.6 28.8 %pool.1 = (bf16[32,3,16,512]{3,2,1,0:T(8,128)(2,1)}, bf16[2816,128]{1,0:T(8,128)(2,1)}, bf16[544,256]{1,0:T(8,128)(2,1)}, bf16[512,512]{1,0:T(8,128)(2,1)}, bf16...) custom-call(s32[8]{0:T(128)} %ids_ref.1, bf16[80,32,128]{2,1,0:T(8,128)(2,1)} %bitcast.9, ...), custom_call_target="tpu_custom_call" | custom-call | tf_op jit(solution)/shard_map/pool/pallas_call | solution.py:593
  29.4 33.4 %windows.1 = (bf16[32,3,16,512]{3,2,1,0:T(8,128)(2,1)}, bf16[2,8,176,128]{3,2,1,0:T(8,128)(2,1)}) custom-call(bf16[2,8,176,128]{3,2,1,0:T(8,128)(2,1)} %bitcast.8, bf16[8,80,512]{2,1,0:T(8,128)(2,1)} %get-tuple-element.17.xh_ref, bf16[32,3,16,512]{3,2,1,0:T(8,128)(2,1)} %get-tuple-element.18.latent_hbm, bf16[544,256]{1,0:T(8,128)(2,1)} %get-tuple-element.19.w2_ref, ...), custom_call_target="tpu_custom_call" | custom-call | tf_op jit(solution)/shard_map/windows/pallas_call | solution.py:626
  62.8 4.9 %finish.1 = (bf16[32,3,16,512]{3,2,1,0:T(8,128)(2,1)}, f32[80,512]{1,0:T(8,128)}, f32[512,1024]{1,0:T(8,128)}, f32[512,512]{1,0:T(8,128)}) custom-call(bf16[32,3,16,512]{3,2,1,0:T(8,128)(2,1)} %get-tuple-element.21.done_ref, bf16[2816,128]{1,0:T(8,128)(2,1)} %bitcast.7, bf16[128,512]{1,0:T(8,128)(2,1)} %get-tuple-element.23.we_ref, ...), custom_call_target="tpu_custom_call" | custom-call | tf_op jit(solution)/shard_map/finish/pallas_call | solution.py:654
